TPU v7x, 32 devices: a whole 2x2x4 slice. The times are simulated.
32 devices in a mesh: dp: 8 (over z, y), shard: 4 (over x, core).
Axes of the slice: x: 2, y: 2, z: 4, core: 2. Of those that a mesh axis runs over, the one named last changes fastest.
Arguments:
- tokens: bfloat16 [32768, 512], P(('dp', 'shard')), may hold values from -6 to 6
- memory: bfloat16 [32768, 512], P(('dp', 'shard')), may hold values from -6 to 6
- target_lengths: int32 [32, 16], P(('dp', 'shard')), may hold values from 1 to 512, 1024 in all within a row
- source_lengths: int32 [32, 16], P(('dp', 'shard')), may hold values from 1 to 512, 1024 in all within a row
- out_grad: bfloat16 [32768, 512], P(('dp', 'shard')), may hold values from -6 to 6
- weights: float32 [4, 512, 2048], P(None, ('dp', 'shard')), may hold values from -1 to 1
- vectors: float32 [17, 512], P(None, ('dp', 'shard')), may hold values from -1 to 3
- weight_moments: float32 [2, 4, 512, 2048], P(None, None, ('dp', 'shard')), may hold values from -1 to 1, as said below
- vector_moments: float32 [2, 17, 512], P(None, None, ('dp', 'shard')), may hold values from -1 to 1, as said below
Outputs:
- layer_out: bfloat16 [32768, 512], P(('dp', 'shard'))
- input_grad: float32 [32768, 512], P(('dp', 'shard'))
- memory_grad: float32 [32768, 512], P(('dp', 'shard'))
- grad_norm: float32 [], replicated
- weight_grads: float32 [4, 512, 2048], P(None, ('dp', 'shard'))
- vector_grads: float32 [17, 512], P(None, ('dp', 'shard'))
- weight_steps: float32 [4, 512, 2048], P(None, ('dp', 'shard'))
- vector_steps: float32 [17, 512], P(None, ('dp', 'shard'))
- new_weight_first: float32 [4, 512, 2048], P(None, ('dp', 'shard'))
- new_weight_second: float32 [4, 512, 2048], P(None, ('dp', 'shard'))
- new_vector_first: float32 [17, 512], P(None, ('dp', 'shard'))
- new_vector_second: float32 [17, 512], P(None, ('dp', 'shard'))
Inputs may be any that keep to these rules, and one draw needn't show every extreme that they name: `target_lengths`: the lengths of each packed row sum to 1024; target sentence i of a row is the translation of source sentence i of the same row. `source_lengths`: the lengths of each packed row sum to 1024. `weight_moments`: the second moments, index 1 of the first dimension, are not negative. `vector_moments`: the second moments, index 1 of the first dimension, are not negative.
All inputs are finite; a program needn't handle non-finite values.
Results may differ from a plain program's by a relative error of at most 0.018.
The roundings to bfloat16 on the way count: a program that leaves them out, or rounds other values in their place, can miss the bound.
Values may be sent and summed in bfloat16 or wider, within the bound.
A program may use at most 192 MiB of HBM per device.

v0:
```python
import jax
import jax.numpy as jnp
from jax import lax
from jax.sharding import PartitionSpec as P

H = 8
HD = 64
ROW_LEN = 1024


EPSILON = 1e-05
MASKED = -1000000000.0
CLIP_NORM = 1.0
LEARN_RATE = 0.001
BETA_ONE = 0.9
BETA_TWO = 0.999
ADAM_EPS = 1e-08
WEIGHT_DECAY = 0.1
CORRECT_ONE = 1.0 - 0.9**3
CORRECT_TWO = 1.0 - 0.999**3


def fetch_forward(matrices, vec_rows):
    return (
        lax.all_gather(matrices.astype(jnp.bfloat16), ("dp", "shard"), axis=1, tiled=True),
        lax.all_gather(vec_rows.astype(jnp.bfloat16), ("dp", "shard"), axis=1, tiled=True),
    )


def fetch_backward(matrices, vec_rows):
    return (
        lax.all_gather(matrices.astype(jnp.bfloat16), ("dp", "shard"), axis=1, tiled=True),
        lax.all_gather(vec_rows.astype(jnp.bfloat16), ("dp", "shard"), axis=1, tiled=True),
    )


def tokens_dot(left, right):
    return lax.dot_general(
        left, right, (((0,), (0,)), ((), ())), preferred_element_type=jnp.float32
    )


def back_dot(left, right):
    return lax.dot_general(
        left, right, (((1,), (1,)), ((), ())), preferred_element_type=jnp.float32
    )


def norm_forward(inputs, gain_row, bias_row):
    centred = inputs - jnp.mean(inputs, axis=-1, keepdims=True)
    inverse = lax.rsqrt(jnp.mean(centred * centred, axis=-1, keepdims=True) + EPSILON)
    normed = centred * inverse
    return (normed * gain_row + bias_row, normed, inverse)


def norm_backward(grad_in, normed, inverse, gain_row):
    gain_grad = jnp.sum(grad_in * normed, axis=0)
    bias_grad = jnp.sum(grad_in, axis=0)
    scaled = grad_in * gain_row
    value_grad = inverse * (
        scaled
        - jnp.mean(scaled, axis=-1, keepdims=True)
        - normed * jnp.mean(scaled * normed, axis=-1, keepdims=True)
    )
    return (value_grad, gain_grad, bias_grad)


def segment_ids(lengths, row_len):
    sentence_ends = jnp.cumsum(lengths, axis=-1)
    places = lax.iota(jnp.int32, row_len)
    return jnp.sum((sentence_ends[:, None, :] <= places[None, :, None]).astype(jnp.int32), axis=-1)


def block_scores(
    queries, key_rows, query_seg, key_seg, causal, block_index, blocks_per_row, query_block
):
    row_index = block_index // blocks_per_row
    row_start = block_index % blocks_per_row * query_block
    query_part = lax.dynamic_slice_in_dim(
        lax.dynamic_index_in_dim(queries, row_index, 0, False), row_start, query_block, 0
    )
    key_part = lax.dynamic_index_in_dim(key_rows, row_index, 0, False)
    query_ids = lax.dynamic_slice_in_dim(
        lax.dynamic_index_in_dim(query_seg, row_index, 0, False), row_start, query_block, 0
    )
    key_ids = lax.dynamic_index_in_dim(key_seg, row_index, 0, False)
    allowed = query_ids[:, None] == key_ids[None, :]
    if causal:
        query_pos = row_start + lax.iota(jnp.int32, query_block)
        key_pos = lax.iota(jnp.int32, key_ids.shape[0])
        allowed = allowed & (key_pos[None, :] <= query_pos[:, None])
    score_scale = queries.shape[-1] ** (-0.5)
    scores = (
        jnp.einsum("qhd,khd->hqk", query_part, key_part, preferred_element_type=jnp.float32)
        * score_scale
    )
    scores = jnp.where(allowed[None], scores, MASKED)
    return (scores, query_part, row_index, row_start)


def attend_forward(queries, key_rows, value_rows, query_seg, key_seg, causal):
    row_count, seq_len, head_count, head_size = queries.shape
    query_block = min(512, seq_len)
    blocks_per_row = seq_len // query_block

    def block_step(block_index):
        scores, query_part, row_index, row_start = block_scores(
            queries, key_rows, query_seg, key_seg, causal, block_index, blocks_per_row, query_block
        )
        value_part = lax.dynamic_index_in_dim(value_rows, row_index, 0, False)
        row_max = jnp.max(scores, axis=-1, keepdims=True)
        shifted = jnp.exp(scores - row_max)
        exp_total = jnp.sum(shifted, axis=-1, keepdims=True)
        soft_weights = (shifted / exp_total).astype(jnp.bfloat16)
        outputs = jnp.einsum(
            "hqk,khd->qhd", soft_weights, value_part, preferred_element_type=jnp.float32
        )
        return (outputs.astype(jnp.bfloat16), (row_max + jnp.log(exp_total))[..., 0])

    outputs, lse_rows = lax.map(block_step, jnp.arange(row_count * blocks_per_row, dtype=jnp.int32))
    return (outputs.reshape(row_count * seq_len, head_count * head_size), lse_rows)


def attend_backward(queries, key_rows, value_rows, query_seg, key_seg, causal, grad_rows, lse_rows):
    row_count, seq_len, head_count, head_size = queries.shape
    query_block = min(512, seq_len)
    blocks_per_row = seq_len // query_block
    score_scale = head_size ** (-0.5)

    def block_step(carried, block_index):
        key_acc, value_acc = carried
        scores, query_part, row_index, row_start = block_scores(
            queries, key_rows, query_seg, key_seg, causal, block_index, blocks_per_row, query_block
        )
        key_part = lax.dynamic_index_in_dim(key_rows, row_index, 0, False)
        value_part = lax.dynamic_index_in_dim(value_rows, row_index, 0, False)
        grad_part = lax.dynamic_slice_in_dim(
            lax.dynamic_index_in_dim(grad_rows, row_index, 0, False), row_start, query_block, 0
        )
        lse_part = lax.dynamic_index_in_dim(lse_rows, block_index, 0, False)
        soft_weights = jnp.exp(scores - lse_part[..., None])
        low_weights = soft_weights.astype(jnp.bfloat16)
        soft_grads = jnp.einsum(
            "qhd,khd->hqk", grad_part, value_part, preferred_element_type=jnp.float32
        )
        row_dot = jnp.sum(soft_weights * soft_grads, axis=-1, keepdims=True)
        score_grads = (soft_weights * (soft_grads - row_dot)).astype(jnp.bfloat16)
        query_grad = (
            jnp.einsum("hqk,khd->qhd", score_grads, key_part, preferred_element_type=jnp.float32)
            * score_scale
        )
        key_grad = (
            jnp.einsum("hqk,qhd->khd", score_grads, query_part, preferred_element_type=jnp.float32)
            * score_scale
        )
        value_grad = jnp.einsum(
            "hqk,qhd->khd", low_weights, grad_part, preferred_element_type=jnp.float32
        )
        key_acc = lax.dynamic_update_index_in_dim(
            key_acc, lax.dynamic_index_in_dim(key_acc, row_index, 0, False) + key_grad, row_index, 0
        )
        value_acc = lax.dynamic_update_index_in_dim(
            value_acc,
            lax.dynamic_index_in_dim(value_acc, row_index, 0, False) + value_grad,
            row_index,
            0,
        )
        return ((key_acc, value_acc), query_grad)

    zero_grads = jnp.zeros(key_rows.shape, jnp.float32)
    (key_acc, value_acc), query_grads = lax.scan(
        block_step,
        (zero_grads, zero_grads),
        jnp.arange(row_count * blocks_per_row, dtype=jnp.int32),
    )
    flat_shape = (row_count * seq_len, head_count * head_size)
    return (
        query_grads.reshape(flat_shape).astype(jnp.bfloat16),
        key_acc.reshape(flat_shape).astype(jnp.bfloat16),
        value_acc.reshape(flat_shape).astype(jnp.bfloat16),
    )


def adam_update(params, grad_in, moments, factor):
    clipped = factor * grad_in
    first_m = BETA_ONE * moments[0] + (1.0 - BETA_ONE) * clipped
    second_m = BETA_TWO * moments[1] + (1.0 - BETA_TWO) * clipped * clipped
    stepped = first_m / CORRECT_ONE / (jnp.sqrt(second_m / CORRECT_TWO) + ADAM_EPS)
    return (-LEARN_RATE * (stepped + WEIGHT_DECAY * params), first_m, second_m)


def column_sum(values_in):
    return jnp.sum(values_in.astype(jnp.float32), axis=0)


def body(
    tokens,
    memory,
    target_lengths,
    source_lengths,
    out_grad,
    weights,
    vectors,
    weight_moments,
    vector_moments,
):
    token_count, model_width = tokens.shape
    row_count = token_count // ROW_LEN
    target_ids = segment_ids(target_lengths, ROW_LEN)
    source_ids = segment_ids(source_lengths, ROW_LEN)

    def heads_of(flat):
        return flat.reshape(row_count, ROW_LEN, H, HD)

    self_mats, self_vecs = fetch_forward(weights[0:1], vectors[0:5])
    self_weight = self_mats[0]
    self_bias = self_vecs.astype(jnp.float32)
    projected = jnp.dot(
        tokens, self_weight[:, : 3 * model_width], preferred_element_type=jnp.float32
    )
    self_query = (projected[:, :model_width] + self_bias[0]).astype(jnp.bfloat16)
    self_keys = projected[:, model_width : 2 * model_width].astype(jnp.bfloat16)
    self_values = (projected[:, 2 * model_width :] + self_bias[1]).astype(jnp.bfloat16)
    self_attn, self_lse = attend_forward(
        heads_of(self_query),
        heads_of(self_keys),
        heads_of(self_values),
        target_ids,
        target_ids,
        True,
    )
    self_branch = (
        jnp.dot(self_attn, self_weight[:, 3 * model_width :], preferred_element_type=jnp.float32)
        + self_bias[2]
    )
    first_out, first_norm, first_inv = norm_forward(
        tokens.astype(jnp.float32) + self_branch, self_bias[3], self_bias[4]
    )
    first_low = first_out.astype(jnp.bfloat16)
    cross_mats, cross_vecs = fetch_forward(weights[1:2], vectors[5:10])
    cross_weight = cross_mats[0]
    cross_bias = cross_vecs.astype(jnp.float32)
    cross_query = (
        jnp.dot(first_low, cross_weight[:, :model_width], preferred_element_type=jnp.float32)
        + cross_bias[0]
    ).astype(jnp.bfloat16)
    cross_kv = jnp.dot(
        memory, cross_weight[:, model_width : 3 * model_width], preferred_element_type=jnp.float32
    )
    cross_keys = cross_kv[:, :model_width].astype(jnp.bfloat16)
    cross_values = (cross_kv[:, model_width:] + cross_bias[1]).astype(jnp.bfloat16)
    cross_attn, cross_lse = attend_forward(
        heads_of(cross_query),
        heads_of(cross_keys),
        heads_of(cross_values),
        target_ids,
        source_ids,
        False,
    )
    cross_branch = (
        jnp.dot(cross_attn, cross_weight[:, 3 * model_width :], preferred_element_type=jnp.float32)
        + cross_bias[2]
    )
    second, second_norm, second_inv = norm_forward(
        first_out + cross_branch, cross_bias[3], cross_bias[4]
    )
    second_low = second.astype(jnp.bfloat16)
    ffn_mats, ffn_vecs = fetch_forward(weights[2:4], vectors[10:17])
    ffn_bias = ffn_vecs.astype(jnp.float32)
    pre_hidden = jnp.dot(second_low, ffn_mats[0], preferred_element_type=jnp.float32) + ffn_bias[
        0:4
    ].reshape(4 * model_width)
    hidden = jax.nn.silu(pre_hidden).astype(jnp.bfloat16)
    ffn_out = back_dot(hidden, ffn_mats[1]) + ffn_bias[4]
    result, third_norm, third_inv = norm_forward(second + ffn_out, ffn_bias[5], ffn_bias[6])
    layer_out = result.astype(jnp.bfloat16)
    ffn_mats, ffn_vecs = fetch_backward(weights[2:4], vectors[10:17])
    ffn_bias = ffn_vecs.astype(jnp.float32)
    grad_out = out_grad.astype(jnp.float32)
    third_grad, gain_three, bias_three = norm_backward(grad_out, third_norm, third_inv, ffn_bias[5])
    ffn_grad = third_grad.astype(jnp.bfloat16)
    down_grad = tokens_dot(ffn_grad, hidden)
    hidden_grad = jnp.dot(ffn_grad, ffn_mats[1], preferred_element_type=jnp.float32)
    gate_sig = jax.nn.sigmoid(pre_hidden)
    pre_grad = (hidden_grad * gate_sig * (1.0 + pre_hidden * (1.0 - gate_sig))).astype(jnp.bfloat16)
    up_grad = tokens_dot(second_low, pre_grad)
    second_grad = third_grad + back_dot(pre_grad, ffn_mats[0])
    ffn_mat_grads = jnp.stack([up_grad, down_grad])
    ffn_vec_grads = jnp.concatenate(
        [
            column_sum(pre_grad).reshape(4, model_width),
            jnp.stack([column_sum(ffn_grad), gain_three, bias_three]),
        ],
        axis=0,
    )
    cross_mats, cross_vecs = fetch_backward(weights[1:2], vectors[5:10])
    cross_weight = cross_mats[0]
    cross_bias = cross_vecs.astype(jnp.float32)
    second_in_grad, gain_two, bias_two = norm_backward(
        second_grad, second_norm, second_inv, cross_bias[3]
    )
    cross_branch_grad = second_in_grad.astype(jnp.bfloat16)
    cross_out_grad = tokens_dot(cross_attn, cross_branch_grad)
    cross_attn_grad = back_dot(cross_branch_grad, cross_weight[:, 3 * model_width :]).astype(
        jnp.bfloat16
    )
    cross_query_grad, cross_keys_grad, cross_values_grad = attend_backward(
        heads_of(cross_query),
        heads_of(cross_keys),
        heads_of(cross_values),
        target_ids,
        source_ids,
        False,
        heads_of(cross_attn_grad),
        cross_lse,
    )
    cross_kv_grad = jnp.concatenate([cross_keys_grad, cross_values_grad], axis=1)
    cross_qw_grad = tokens_dot(first_low, cross_query_grad)
    cross_kvw_grad = tokens_dot(memory, cross_kv_grad)
    memory_grad = back_dot(cross_kv_grad, cross_weight[:, model_width : 3 * model_width])
    first_grad = second_in_grad + back_dot(cross_query_grad, cross_weight[:, :model_width])
    cross_mat_grads = jnp.concatenate([cross_qw_grad, cross_kvw_grad, cross_out_grad], axis=1)[None]
    cross_vec_grads = jnp.stack(
        [
            column_sum(cross_query_grad),
            column_sum(cross_values_grad),
            column_sum(cross_branch_grad),
            gain_two,
            bias_two,
        ]
    )
    self_mats, self_vecs = fetch_backward(weights[0:1], vectors[0:5])
    self_weight = self_mats[0]
    self_bias = self_vecs.astype(jnp.float32)
    first_in_grad, gain_one, bias_one = norm_backward(
        first_grad, first_norm, first_inv, self_bias[3]
    )
    self_branch_grad = first_in_grad.astype(jnp.bfloat16)
    self_out_grad = tokens_dot(self_attn, self_branch_grad)
    self_attn_grad = back_dot(self_branch_grad, self_weight[:, 3 * model_width :]).astype(
        jnp.bfloat16
    )
    self_query_grad, self_keys_grad, self_values_grad = attend_backward(
        heads_of(self_query),
        heads_of(self_keys),
        heads_of(self_values),
        target_ids,
        target_ids,
        True,
        heads_of(self_attn_grad),
        self_lse,
    )
    self_qkv_grad = jnp.concatenate([self_query_grad, self_keys_grad, self_values_grad], axis=1)
    self_qkvw_grad = tokens_dot(tokens, self_qkv_grad)
    input_grad = first_in_grad + back_dot(self_qkv_grad, self_weight[:, : 3 * model_width])
    self_mat_grads = jnp.concatenate([self_qkvw_grad, self_out_grad], axis=1)[None]
    self_vec_grads = jnp.stack(
        [
            column_sum(self_query_grad),
            column_sum(self_values_grad),
            column_sum(self_branch_grad),
            gain_one,
            bias_one,
        ]
    )
    mat_share, vec_share = (
        lax.psum_scatter(
            jnp.concatenate([self_mat_grads, cross_mat_grads, ffn_mat_grads], axis=0),
            ("dp", "shard"),
            scatter_dimension=1,
            tiled=True,
        ),
        lax.psum_scatter(
            jnp.concatenate([self_vec_grads, cross_vec_grads, ffn_vec_grads], axis=0),
            ("dp", "shard"),
            scatter_dimension=1,
            tiled=True,
        ),
    )
    local_squares = jnp.sum(mat_share * mat_share) + jnp.sum(vec_share * vec_share)
    grad_total = lax.psum(local_squares, ("dp", "shard"))
    grad_norm = jnp.sqrt(grad_total)
    factor = jnp.minimum(1.0, CLIP_NORM / (grad_norm + 1e-06))
    weight_steps, weight_first, weight_second = adam_update(
        weights, mat_share, weight_moments, factor
    )
    vector_steps, vector_first, vector_second = adam_update(
        vectors, vec_share, vector_moments, factor
    )
    return (
        layer_out,
        input_grad,
        memory_grad,
        grad_norm,
        mat_share,
        vec_share,
        weight_steps,
        vector_steps,
        weight_first,
        weight_second,
        vector_first,
        vector_second,
    )


def solution(mesh):
    return jax.shard_map(
        body,
        mesh=mesh,
        in_specs=(
            P(("dp", "shard"), None),
            P(("dp", "shard"), None),
            P(("dp", "shard"), None),
            P(("dp", "shard"), None),
            P(("dp", "shard"), None),
            P(None, ("dp", "shard"), None),
            P(None, ("dp", "shard")),
            P(None, None, ("dp", "shard"), None),
            P(None, None, ("dp", "shard")),
        ),
        out_specs=(
            P(("dp", "shard"), None),
            P(("dp", "shard"), None),
            P(("dp", "shard"), None),
            P(),
            P(None, ("dp", "shard"), None),
            P(None, ("dp", "shard")),
            P(None, ("dp", "shard"), None),
            P(None, ("dp", "shard")),
            P(None, ("dp", "shard"), None),
            P(None, ("dp", "shard"), None),
            P(None, ("dp", "shard")),
            P(None, ("dp", "shard")),
        ),
        check_vma=False,
    )
```

profile of v0, /device:TPU:0, one launch (start us, length us, event | category | flops | bytes accessed | tf_op | source)
XLA Modules:
  0.0 1024.2 jit_solution(17621650155734772995)
XLA Ops:
  12.1 43.4 %all-gather.2 = bf16[32,16,7]{1,2,0:T(8,128)(2,1)S(1)} all-gather(bf16[1,16,7]{1,2,0:T(8,128)(2,1)S(1)} %slice_bitcast_fusion.11), channel_id=1, replica_groups=mesh['dp'=8,'shard'=4] {'dp','shard'}, dimensions={0}, use_global_device_ids=true | all-gather | bytes 7392 | tf_op jit(solution)/shard_map/all_gather | solution.py:26
  56.4 36.8 %all-gather = bf16[32,16,5]{1,2,0:T(8,128)(2,1)S(1)} all-gather(bf16[1,16,5]{1,2,0:T(8,128)(2,1)S(1)} %get-tuple-element.752), channel_id=1, replica_groups=mesh['dp'=8,'shard'=4] {'dp','shard'}, dimensions={0}, use_global_device_ids=true | all-gather | bytes 5280 | tf_op jit(solution)/shard_map/all_gather | solution.py:26
  95.7 38.4 %all-gather.1 = bf16[32,16,5]{1,2,0:T(8,128)(2,1)S(1)} all-gather(bf16[1,16,5]{1,2,0:T(8,128)(2,1)S(1)} %get-tuple-element.751), channel_id=1, replica_groups=mesh['dp'=8,'shard'=4] {'dp','shard'}, dimensions={0}, use_global_device_ids=true | all-gather | bytes 5280 | tf_op jit(solution)/shard_map/all_gather | solution.py:26
  137.9 3.2 fusion.95
  149.8 35.7 %while.60 = (s32[]{:T(128)}, bf16[2,512,8,64]{1,3,2,0:T(8,128)(2,1)}, f32[2,8,512]{2,1,0:T(8,128)}, s32[2]{0:T(128)S(1)}, s32[1,1024]{1,0:T(1,128)S(1)}, /*index...) while((s32[]{:T(128)}, ...), condition=%wide.region_5.6_spmd, body=%wide.region_2.0_spmd.sunk | while | flops 1125904896 | bytes 55721264 | solution.py:120
  153.0 3.0 fusion.196
  156.0 4.2 fusion.197
  160.9 6.6 fusion.198
  170.6 3.0 fusion.196
  173.6 4.2 fusion.197
  178.5 6.6 fusion.198
  185.6 3.1 copy.161
  191.5 2.9 fusion.99
  197.5 2.9 add_convert_fusion.1
  200.5 36.1 %while.61 = (s32[]{:T(128)}, bf16[2,512,8,64]{1,3,2,0:T(8,128)(2,1)S(1)}, f32[2,8,512]{2,1,0:T(8,128)S(1)}, s32[2]{0:T(128)S(1)}, s32[1,1024]{1,0:T(1,128)S(1)},...) while((s32[]{:T(128)}, ...), condition=%wide.region_13.14_spmd, body=%wide.region_10.13_spmd.sunk | while | flops 1124855808 | bytes 55716156 | solution.py:120
  203.4 4.9 fusion.200
  208.3 4.2 fusion.201
  212.6 5.9 fusion.202
  221.4 4.8 fusion.200
  226.3 4.2 fusion.201
  230.6 5.9 fusion.202
  241.3 5.6 multiply_convert_fusion.3
  254.7 6.0 convert_reduce_fusion
  260.8 4.1 multiply_reduce_fusion.2
  266.2 3.2 convolution_convert_fusion.1
  273.7 116.8 %while.62 = (s32[]{:T(128)}, f32[1,1024,8,64]{1,3,2,0:T(8,128)}, f32[1,1024,8,64]{1,3,2,0:T(8,128)}, bf16[2,512,8,64]{1,3,2,0:T(8,128)(2,1)}, s32[2]{0:T(128)S(1...) while((s32[]{:T(128)}, f32[1,1024,8,64]{1,3,2,0:T(8,128)}, ...), condition=%wide.region_24.25_spmd, body=%wide.region_22.24_spmd.sunk | while | flops 2724458496 | bytes 301296256 | solution.py:171
  276.7 9.5 fusion.211
  289.3 15.8 %multiply_reduce_fusion.15 = (f32[8,512]{1,0:T(8,128)}, f32[8,512,1024]{2,1,0:T(8,128)}) fusion(f32[8,512,1024]{2,1,0:T(8,128)} %fusion.211, f32[8,512]{1,0:T(8,128)} %dynamic-slice_bitcast_fusion.4, bf16[1,1024,8,64]{1,3,2,0:T(8,128)(2,1)} %get-tuple-element.1150, bf16[1,1024,8,64]{1,3,2,0:T(8,128)(2,1)} %get-tuple-element.1147, ...), kind=kOutput, calls=%fused_computation.43.clone.1 | convolution fusion | flops 557838336 | bytes 35684356 | tf_op jit(solution)/shard_map/while/body/eval_jaxpr/qhd,khd->hqk/dot_general | solution.py:94
  306.3 6.8 multiply_convert_fusion.6
  313.2 6.9 fusion.212
  320.1 7.0 fusion.214
  327.2 5.1 fusion.213
  334.8 9.5 fusion.211
  347.4 15.8 %multiply_reduce_fusion.15 = (f32[8,512]{1,0:T(8,128)}, f32[8,512,1024]{2,1,0:T(8,128)}) fusion(f32[8,512,1024]{2,1,0:T(8,128)} %fusion.211, f32[8,512]{1,0:T(8,128)} %dynamic-slice_bitcast_fusion.4, bf16[1,1024,8,64]{1,3,2,0:T(8,128)(2,1)} %get-tuple-element.1150, bf16[1,1024,8,64]{1,3,2,0:T(8,128)(2,1)} %get-tuple-element.1147, ...), kind=kOutput, calls=%fused_computation.43.clone.1 | convolution fusion | flops 557838336 | bytes 35684356 | tf_op jit(solution)/shard_map/while/body/eval_jaxpr/qhd,khd->hqk/dot_general | solution.py:94
  364.5 6.8 multiply_convert_fusion.6
  371.4 7.0 fusion.212
  378.3 7.0 fusion.214
  385.4 5.1 fusion.213
  394.6 3.0 multiply_reduce_fusion.3
  399.0 3.1 convolution_convert_fusion
  406.3 117.8 %while.63 = (s32[]{:T(128)}, f32[1,1024,8,64]{1,3,2,0:T(8,128)}, f32[1,1024,8,64]{1,3,2,0:T(8,128)}, bf16[2,512,8,64]{1,3,2,0:T(8,128)(2,1)}, s32[2]{0:T(128)S(1...) while((s32[]{:T(128)}, f32[1,1024,8,64]{1,3,2,0:T(8,128)}, ...), condition=%wide.region_29.30_spmd, body=%wide.region_27.29_spmd.sunk | while | flops 2725507584 | bytes 301038656 | solution.py:171
  409.0 9.5 fusion.223
  422.6 15.8 %multiply_reduce_fusion.16 = (f32[8,512]{1,0:T(8,128)}, f32[8,512,1024]{2,1,0:T(8,128)}) fusion(f32[8,512,1024]{2,1,0:T(8,128)} %fusion.223, f32[8,512]{1,0:T(8,128)} %dynamic-slice_bitcast_fusion.5, bf16[1,1024,8,64]{1,3,2,0:T(8,128)(2,1)} %get-tuple-element.1198, bf16[1,1024,8,64]{1,3,2,0:T(8,128)(2,1)} %get-tuple-element.1196, ...), kind=kOutput, calls=%fused_computation.74.clone.1 | convolution fusion | flops 557838336 | bytes 35684356 | tf_op jit(solution)/shard_map/while/body/eval_jaxpr/qhd,khd->hqk/dot_general | solution.py:94
  439.7 6.9 multiply_convert_fusion.7
  446.6 6.3 fusion.225
  452.9 7.6 fusion.227
  460.5 4.7 fusion.226
  467.8 9.5 fusion.223
  481.3 15.8 %multiply_reduce_fusion.16 = (f32[8,512]{1,0:T(8,128)}, f32[8,512,1024]{2,1,0:T(8,128)}) fusion(f32[8,512,1024]{2,1,0:T(8,128)} %fusion.223, f32[8,512]{1,0:T(8,128)} %dynamic-slice_bitcast_fusion.5, bf16[1,1024,8,64]{1,3,2,0:T(8,128)(2,1)} %get-tuple-element.1198, bf16[1,1024,8,64]{1,3,2,0:T(8,128)(2,1)} %get-tuple-element.1196, ...), kind=kOutput, calls=%fused_computation.74.clone.1 | convolution fusion | flops 557838336 | bytes 35684356 | tf_op jit(solution)/shard_map/while/body/eval_jaxpr/qhd,khd->hqk/dot_general | solution.py:94
  498.4 6.9 multiply_convert_fusion.7
  505.3 6.3 fusion.225
  511.7 7.6 fusion.227
  519.3 4.7 fusion.226
  525.8 3.3 copy.172
  534.8 6.9 convolution_bitcast_fusion.2
  541.7 4.5 convolution_bitcast_fusion.1
  565.0 6.3 pad_maximum_fusion
  571.3 20.2 %copy.176 = f32[4,512,2048]{2,0,1:T(4,128)} copy(f32[4,512,2048]{1,2,0:T(8,128)} %pad_maximum_fusion) | data formatting | bytes 33554432 | tf_op jit(solution)/shard_map/concatenate | solution.py:368
  594.7 5.4 convolution_add_fusion.1
  600.1 2.9 copy.184
  603.0 4.6 fusion.97
  607.6 73.0 %reduce-scatter.4.cloned.1.call-done = f32[16,17]{1,0:T(8,128)} async-done(((f32[512,17]{1,0:T(8,128)}), f32[16,17]{1,0:T(8,128)}) %reduce-scatter.4.cloned.1.call-update) | async-done | bytes 1104
  682.0 279.5 %all-reduce.3.cloned.1.call-done = f32[4,512,2048]{2,0,1:T(4,128)} async-done(((f32[4,512,2048]{2,0,1:T(4,128)}), f32[4,512,2048]{2,0,1:T(4,128)}) %all-reduce.3.cloned.1.call-update) | async-done | bytes 16777232
  966.1 40.1 %psum.7 = f32[]{:T(128)} all-reduce(f32[]{:T(128)S(6)} %add.464), channel_id=1, replica_groups=mesh['dp'=8,'shard'=4] {'dp','shard'}, use_global_device_ids=true, to_apply=%region_48.49 | all-reduce | flops 1 | bytes 8 | tf_op jit(solution)/shard_map/psum | solution.py:381
  (422 shorter events, 119.0 us)
Async XLA Ops:
  7.2 184.4 %copy-start = (bf16[1024,512]{1,0:T(8,128)(2,1)S(1)}, bf16[1024,512]{1,0:T(8,128)(2,1)}, u32[]{:S(2)}) copy-start(bf16[1024,512]{1,0:T(8,128)(2,1)} %param.18) | copy-start | bytes 3145732
  7.2 86.9 %copy-start.97 = (s32[1,16]{1,0:T(1,128)S(1)}, s32[1,16]{1,0:T(1,128)}, u32[]{:S(2)}) copy-start(s32[1,16]{1,0:T(1,128)} %param.19) | copy-start | bytes 196
  7.2 87.2 %copy-start.41 = (bf16[1024,512]{1,0:T(8,128)(2,1)S(1)}, bf16[1024,512]{1,0:T(8,128)(2,1)}, u32[]{:S(2)}) copy-start(bf16[1024,512]{1,0:T(8,128)(2,1)} %param.17) | copy-start | bytes 3145732
  7.2 130.7 %all-gather.7.cloned.1.call-start = ((), (), s32[]{:S(2)}) async-start(), calls=%async_computation.1 | async-start | bytes 2162688 | tf_op jit(solution)/shard_map/all_gather | solution.py:25
  8.5 126.6 %copy-start.98 = (s32[1,16]{1,0:T(1,128)S(1)}, s32[1,16]{1,0:T(1,128)}, u32[]{:S(2)}) copy-start(s32[1,16]{1,0:T(1,128)} %param.20) | copy-start | bytes 196
  8.5 128.1 %copy-start.40 = (bf16[1024,512]{1,0:T(8,128)(2,1)S(1)}, bf16[1024,512]{1,0:T(8,128)(2,1)}, u32[]{:S(2)}) copy-start(bf16[1024,512]{1,0:T(8,128)(2,1)} %param.21) | copy-start | bytes 3145732
  9.2 182.3 %all-gather.9.cloned.1.call-start = ((), (), s32[]{:S(2)}) async-start(), calls=%async_computation.2 | async-start | bytes 2162688 | tf_op jit(solution)/shard_map/all_gather | solution.py:25
  9.9 231.0 %all-gather.11.cloned.1.call-start = ((), (), s32[]{:S(2)}) async-start(), calls=%async_computation.3 | async-start | bytes 4325376 | tf_op jit(solution)/shard_map/all_gather | solution.py:25
  10.7 669.9 %reduce-scatter.4.cloned.1.call-start = ((), (), s32[]{:S(2)}) async-start(), calls=%async_computation.4 | async-start | bytes 270336
  191.2 5.7 copy-start.14
  191.2 5.6 copy-start.57
  191.5 5.3 copy-start.60
  240.5 24.3 %copy-start.24 = (f32[1024,512]{0,1:T(8,128)}, f32[1024,512]{0,1:T(8,128)S(1)}, u32[]{:S(2)}) copy-start(f32[1024,512]{0,1:T(8,128)S(1)} %get-tuple-element.756) | copy-start | bytes 6291460
  240.6 24.3 %copy-start.63 = (f32[1024]{0:T(1024)}, f32[1024]{0:T(1024)S(1)}, u32[]{:S(2)}) copy-start(f32[1024]{0:T(1024)S(1)} %broadcast_multiply_fusion.7) | copy-start | bytes 12292
  240.9 23.9 %copy-start.71 = (f32[1024]{0:T(1024)}, f32[1024]{0:T(1024)S(1)}, u32[]{:S(2)}) copy-start(f32[1024]{0:T(1024)S(1)} %add_rsqrt_fusion.1) | copy-start | bytes 12292
  241.3 5.6 copy-start.93
  241.3 5.6 copy-start.96
  254.7 6.1 copy-start.49
  266.2 4.8 copy-start.11
  274.1 14.5 %copy-start.53 = (f32[2,8,512]{2,1,0:T(8,128)}, f32[2,8,512]{2,1,0:T(8,128)S(1)}, u32[]{:S(2)}) copy-start(f32[2,8,512]{2,1,0:T(8,128)S(1)} %get-tuple-element.1151) | copy-start | bytes 98308 | tf_op jit(solution)/shard_map/while
  289.2 15.8 %slice-start.4 = ((s8[16777216]{0:T(1024)(128)(4,1)}), s8[4194304]{0:T(1024)(128)(4,1)S(1)}, s32[]{:S(2)}) async-start(s8[16777216]{0:T(1024)(128)(4,1)} %bitcast.416), calls=%async_computation.10 | async-start | bytes 8388608 | tf_op jit(solution)/shard_map/while
  289.2 15.8 %slice-start.5 = ((s8[16777216]{0:T(1024)(128)(4,1)}), s8[4194304]{0:T(1024)(128)(4,1)S(1)}, s32[]{:S(2)}) async-start(s8[16777216]{0:T(1024)(128)(4,1)} %bitcast.416), calls=%async_computation.11 | async-start | bytes 8388608 | tf_op jit(solution)/shard_map/while
  289.2 15.8 %slice-start.6 = ((s8[16777216]{0:T(1024)(128)(4,1)}), s8[4194304]{0:T(1024)(128)(4,1)S(1)}, s32[]{:S(2)}) async-start(s8[16777216]{0:T(1024)(128)(4,1)} %bitcast.416), calls=%async_computation.12 | async-start | bytes 8388608 | tf_op jit(solution)/shard_map/while
  289.2 17.1 %slice-start.7 = ((s8[16777216]{0:T(1024)(128)(4,1)}), s8[4194304]{0:T(1024)(128)(4,1)S(1)}, s32[]{:S(2)}) async-start(s8[16777216]{0:T(1024)(128)(4,1)} %bitcast.416), calls=%async_computation.13 | async-start | bytes 8388608 | tf_op jit(solution)/shard_map/while
  313.2 7.0 copy-start.3
  313.2 7.0 copy-start.20
  313.2 14.0 %copy-start.1 = (f32[8,512,1024]{2,1,0:T(8,128)S(1)}, f32[8,512,1024]{2,1,0:T(8,128)}, u32[]{:S(2)}) copy-start(f32[8,512,1024]{2,1,0:T(8,128)} %get-tuple-element.1012) | copy-start | bytes 50331652 | tf_op jit(solution)/shard_map/while
  327.2 5.1 copy-start.21
  327.2 5.1 copy-start.54
  332.3 14.5 %copy-start.53 = (f32[2,8,512]{2,1,0:T(8,128)}, f32[2,8,512]{2,1,0:T(8,128)S(1)}, u32[]{:S(2)}) copy-start(f32[2,8,512]{2,1,0:T(8,128)S(1)} %get-tuple-element.1151) | copy-start | bytes 98308 | tf_op jit(solution)/shard_map/while
  347.4 15.8 %slice-start.4 = ((s8[16777216]{0:T(1024)(128)(4,1)}), s8[4194304]{0:T(1024)(128)(4,1)S(1)}, s32[]{:S(2)}) async-start(s8[16777216]{0:T(1024)(128)(4,1)} %bitcast.416), calls=%async_computation.10 | async-start | bytes 8388608 | tf_op jit(solution)/shard_map/while
  347.4 15.8 %slice-start.5 = ((s8[16777216]{0:T(1024)(128)(4,1)}), s8[4194304]{0:T(1024)(128)(4,1)S(1)}, s32[]{:S(2)}) async-start(s8[16777216]{0:T(1024)(128)(4,1)} %bitcast.416), calls=%async_computation.11 | async-start | bytes 8388608 | tf_op jit(solution)/shard_map/while
  347.4 15.8 %slice-start.6 = ((s8[16777216]{0:T(1024)(128)(4,1)}), s8[4194304]{0:T(1024)(128)(4,1)S(1)}, s32[]{:S(2)}) async-start(s8[16777216]{0:T(1024)(128)(4,1)} %bitcast.416), calls=%async_computation.12 | async-start | bytes 8388608 | tf_op jit(solution)/shard_map/while
  347.4 17.1 %slice-start.7 = ((s8[16777216]{0:T(1024)(128)(4,1)}), s8[4194304]{0:T(1024)(128)(4,1)S(1)}, s32[]{:S(2)}) async-start(s8[16777216]{0:T(1024)(128)(4,1)} %bitcast.416), calls=%async_computation.13 | async-start | bytes 8388608 | tf_op jit(solution)/shard_map/while
  371.3 7.0 copy-start.3
  371.4 7.0 copy-start.20
  371.4 14.0 %copy-start.1 = (f32[8,512,1024]{2,1,0:T(8,128)S(1)}, f32[8,512,1024]{2,1,0:T(8,128)}, u32[]{:S(2)}) copy-start(f32[8,512,1024]{2,1,0:T(8,128)} %get-tuple-element.1012) | copy-start | bytes 50331652 | tf_op jit(solution)/shard_map/while
  385.3 5.1 copy-start.21
  385.4 5.1 copy-start.54
  399.0 4.8 copy-start.17
  422.6 15.8 %slice-start = ((s8[16777216]{0:T(1024)(128)(4,1)}), s8[4194304]{0:T(1024)(128)(4,1)S(1)}, s32[]{:S(2)}) async-start(s8[16777216]{0:T(1024)(128)(4,1)} %bitcast.414), calls=%async_computation.6 | async-start | bytes 8388608 | tf_op jit(solution)/shard_map/while
  422.6 15.8 %slice-start.1 = ((s8[16777216]{0:T(1024)(128)(4,1)}), s8[4194304]{0:T(1024)(128)(4,1)S(1)}, s32[]{:S(2)}) async-start(s8[16777216]{0:T(1024)(128)(4,1)} %bitcast.414), calls=%async_computation.7 | async-start | bytes 8388608 | tf_op jit(solution)/shard_map/while
  422.6 15.8 %slice-start.2 = ((s8[16777216]{0:T(1024)(128)(4,1)}), s8[4194304]{0:T(1024)(128)(4,1)S(1)}, s32[]{:S(2)}) async-start(s8[16777216]{0:T(1024)(128)(4,1)} %bitcast.414), calls=%async_computation.8 | async-start | bytes 8388608 | tf_op jit(solution)/shard_map/while
  422.6 17.1 %slice-start.3 = ((s8[16777216]{0:T(1024)(128)(4,1)}), s8[4194304]{0:T(1024)(128)(4,1)S(1)}, s32[]{:S(2)}) async-start(s8[16777216]{0:T(1024)(128)(4,1)} %bitcast.414), calls=%async_computation.9 | async-start | bytes 8388608 | tf_op jit(solution)/shard_map/while
  439.6 6.9 copy-start.10
  446.6 6.4 copy-start.4
  446.6 6.3 copy-start.6
  446.6 13.9 %copy-start.2 = (f32[8,512,1024]{2,1,0:T(8,128)S(1)}, f32[8,512,1024]{2,1,0:T(8,128)}, u32[]{:S(2)}) copy-start(f32[8,512,1024]{2,1,0:T(8,128)} %get-tuple-element.1025) | copy-start | bytes 50331652 | tf_op jit(solution)/shard_map/while
  481.3 15.8 %slice-start = ((s8[16777216]{0:T(1024)(128)(4,1)}), s8[4194304]{0:T(1024)(128)(4,1)S(1)}, s32[]{:S(2)}) async-start(s8[16777216]{0:T(1024)(128)(4,1)} %bitcast.414), calls=%async_computation.6 | async-start | bytes 8388608 | tf_op jit(solution)/shard_map/while
  481.3 15.8 %slice-start.1 = ((s8[16777216]{0:T(1024)(128)(4,1)}), s8[4194304]{0:T(1024)(128)(4,1)S(1)}, s32[]{:S(2)}) async-start(s8[16777216]{0:T(1024)(128)(4,1)} %bitcast.414), calls=%async_computation.7 | async-start | bytes 8388608 | tf_op jit(solution)/shard_map/while
  481.3 15.8 %slice-start.2 = ((s8[16777216]{0:T(1024)(128)(4,1)}), s8[4194304]{0:T(1024)(128)(4,1)S(1)}, s32[]{:S(2)}) async-start(s8[16777216]{0:T(1024)(128)(4,1)} %bitcast.414), calls=%async_computation.8 | async-start | bytes 8388608 | tf_op jit(solution)/shard_map/while
  481.3 17.1 %slice-start.3 = ((s8[16777216]{0:T(1024)(128)(4,1)}), s8[4194304]{0:T(1024)(128)(4,1)S(1)}, s32[]{:S(2)}) async-start(s8[16777216]{0:T(1024)(128)(4,1)} %bitcast.414), calls=%async_computation.9 | async-start | bytes 8388608 | tf_op jit(solution)/shard_map/while
  498.4 6.9 copy-start.10
  505.3 6.4 copy-start.4
  505.3 6.4 copy-start.6
  505.3 14.0 %copy-start.2 = (f32[8,512,1024]{2,1,0:T(8,128)S(1)}, f32[8,512,1024]{2,1,0:T(8,128)}, u32[]{:S(2)}) copy-start(f32[8,512,1024]{2,1,0:T(8,128)} %get-tuple-element.1025) | copy-start | bytes 50331652 | tf_op jit(solution)/shard_map/while
  524.2 4.9 copy-start.18
  524.2 4.9 copy-start.29
  534.8 6.9 copy-start.50
  534.8 6.9 copy-start.100
  550.5 411.0 %all-reduce.3.cloned.1.call-start = ((), (), s32[]{:S(2)}) async-start(), calls=%async_computation.5 | async-start | bytes 33554432
  603.0 361.7 %copy-start.30 = (bf16[1024,512]{0,1:T(8,128)(2,1)S(1)}, bf16[1024,512]{0,1:T(8,128)(2,1)}, u32[]{:S(2)}) copy-start(bf16[1024,512]{0,1:T(8,128)(2,1)} %get-tuple-element.731) | copy-start | bytes 3145732
  607.6 399.3 %copy-start.56 = (f32[17,16]{1,0:T(8,128)S(1)}, f32[17,16]{1,0:T(8,128)}, u32[]{:S(2)}) copy-start(f32[17,16]{1,0:T(8,128)} %copy-done.55) | copy-start | bytes 3268
  682.0 328.1 %copy-start.37 = (f32[4,16,2048]{2,1,0:T(8,128)S(1)}, f32[4,16,2048]{2,1,0:T(8,128)}, u32[]{:S(2)}) copy-start(f32[4,16,2048]{2,1,0:T(8,128)} %param.22) | copy-start | bytes 1572868
  (69 other events, 145.9 us)
Sparse Core Ops, SparseCore 0:
  11.5 59.2 all-gather.6
  74.2 55.3 all-gather.8
  133.0 60.8 all-gather.10
  550.6 129.9 reduce-scatter.3
  687.5 273.9 all-reduce.2
where the time goes:
time: 1040 us; the launch traced here: 1020 us
  waiting for transfers between devices  353 us (34%)
  matrix products  288 us (28%)
  blocking collectives  159 us (15%)
  local copies, waits for them, and re-layouts  93.2 us (9%)
  other arithmetic  89.3 us (9%)
  loops' own time  22.7 us (2%)
  between operations  18.5 us (2%)
    unnamed x7, waiting for transfers between devices  353 us
    all_gather x3, blocking collectives, fetch_forward(): lax.all_gather(vec_rows.astype(jnp.bfloat16), ('dp', 'shard'), axis=1, ti...  119 us
    dot_general x8, matrix products, block_scores(): jnp.einsum('qhd,khd->hqk', query_part, key_part, preferred_element_type=j...  78.9 us
    psum x1, blocking collectives, body(): grad_total = lax.psum(local_squares, ('dp', 'shard'))  40.1 us
    dot_general x4, matrix products, block_step(): jnp.einsum('qhd,khd->hqk', grad_part, value_part, preferred_element_type=...  38 us
    dot_general x4, matrix products, block_step(): jnp.einsum('hqk,khd->qhd', score_grads, key_part, preferred_element_type=...  29.2 us
    unnamed x208, local copies, waits for them, and re-layouts  28 us
    convert_element_type x4, other arithmetic, block_step(): score_grads = (soft_weights * (soft_grads - row_dot)).astype(jnp.bfloat16)  27.5 us
  transfers between devices with their start and end apart: 5, of which 2 were waited for; matrix products, arithmetic and copies ran while one was open for 15% of the time, Pallas kernels for 0%

commit v1 on v0

v1 whole, which is shorter than its diff:
```python
import functools
import jax
import jax.numpy as jnp
from jax import lax
from jax.experimental import pallas as pl
from jax.experimental.pallas import tpu as pltpu
from jax.sharding import PartitionSpec as P

HD = 64
EPSILON = 1e-05
MASKED = -1e30
BF = jnp.bfloat16
F32 = jnp.float32
TILE = 256
VROWS = 24
CLIP_NORM = 1.0
LEARN_RATE = 0.001
BETA_ONE = 0.9
BETA_TWO = 0.999
ADAM_EPS = 1e-08
WEIGHT_DECAY = 0.1
CORRECT_ONE = 1.0 - 0.9**3
CORRECT_TWO = 1.0 - 0.999**3


def mm(left, right):
    return jnp.dot(left, right, preferred_element_type=F32)


def mm_t(left, right):
    return lax.dot_general(left, right, (((1,), (1,)), ((), ())), preferred_element_type=F32)


def t_mm(left, right):
    return lax.dot_general(left, right, (((0,), (0,)), ((), ())), preferred_element_type=F32)


def rows_of(i, size=TILE):
    return pl.ds(pl.multiple_of(i * size, size), size)


def normed(z):
    centred = z - jnp.mean(z, axis=-1, keepdims=True)
    inverse = lax.rsqrt(jnp.mean(centred * centred, axis=-1, keepdims=True) + EPSILON)
    return centred * inverse, inverse


def norm_back(grad, n, inverse, gain):
    scaled = grad * gain
    return inverse * (
        scaled
        - jnp.mean(scaled, axis=-1, keepdims=True)
        - n * jnp.mean(scaled * n, axis=-1, keepdims=True)
    )


def fold(values):
    r, c = values.shape
    return jnp.sum(values.astype(F32).reshape(r // 8, 8, c), axis=0)


def heads_join(ref, rows):
    return jnp.concatenate([ref[p, rows, :] for p in range(4)], axis=1)


def heads_split(ref, rows, value):
    for p in range(4):
        ref[p, rows, :] = value[:, p * 128 : (p + 1) * 128]


class Bag:
    pass


def head_mask(h, dtype):
    lane = lax.broadcasted_iota(jnp.int32, (1, 128), 1)
    return jnp.where((lane < HD) if h == 0 else (lane >= HD), 1.0, 0.0).astype(dtype)


def segments(r, lengths, row_ref, col_ref):
    ends = []
    total = jnp.int32(0)
    for s in range(16):
        total = total + lengths[0, s]
        ends.append(total)
    place = lax.broadcasted_iota(jnp.int32, (8, 1024), 1)
    seg = jnp.zeros((8, 1024), jnp.int32)
    for e in ends:
        seg = seg + jnp.where(e <= place, 1, 0)
    row_ref[...] = seg

    def col(i, _):
        at = lax.broadcasted_iota(jnp.int32, (TILE, 128), 0) + i * TILE
        c = jnp.zeros((TILE, 128), jnp.int32)
        for e in ends:
            c = c + jnp.where(e <= at, 1, 0)
        col_ref[rows_of(i), :] = c
        return 0

    lax.fori_loop(0, 4, col, 0)


def attend(r, q_ref, k_ref, v_ref, out_ref, lse_ref, tile, key_start, key_count, bias):
    rows = rows_of(tile)
    keys = pl.ds(key_start, key_count)
    lane = lax.broadcasted_iota(jnp.int32, (TILE, 128), 1)

    def pair(p, lses):
        q = q_ref[p, rows, :]
        k = k_ref[p, keys, :]
        v = v_ref[p, keys, :]
        outs = []
        for h in range(2):
            s = mm_t(q * head_mask(h, BF), k) + bias[:, :key_count]
            top = jnp.max(s, axis=-1, keepdims=True)
            e = jnp.exp(s - top)
            total = jnp.sum(e, axis=-1, keepdims=True)
            outs.append(mm(e.astype(BF), v) * (1.0 / total))
            lses = jnp.where(lane == 2 * p + h, top + jnp.log(total), lses)
        out_ref[p, rows, :] = jnp.where(lane < HD, outs[0], outs[1]).astype(BF)
        return lses

    lses = lax.fori_loop(0, 4, pair, jnp.zeros((TILE, 128), F32))
    flipped = lses.T
    for h in range(8):
        lse_ref[h, :, rows_of(tile)] = flipped[h : h + 1, :]


def deltas(r, out_ref, grad_ref, delta_ref, tile):
    rows = rows_of(tile)
    lane = lax.broadcasted_iota(jnp.int32, (TILE, 128), 1)
    table = jnp.zeros((TILE, 128), F32)
    for p in range(4):
        prod = out_ref[p, rows, :].astype(F32) * grad_ref[p, rows, :].astype(F32)
        for h in range(2):
            one = jnp.sum(prod * head_mask(h, F32), axis=-1, keepdims=True)
            table = jnp.where(lane == 2 * p + h, one, table)
    flipped = table.T
    for h in range(8):
        delta_ref[h, :, rows] = flipped[h : h + 1, :]


def attend_back(r, q_ref, k_ref, v_ref, grad_ref, lse_ref, delta_ref, bias, i, j):
    qr, kr = rows_of(i), rows_of(j)
    lane = lax.broadcasted_iota(jnp.int32, (TILE, 128), 1)

    def pair(p, _):
        q, k, v, g = q_ref[p, qr, :], k_ref[p, kr, :], v_ref[p, kr, :], grad_ref[p, qr, :]
        dv, dk, dq = [], [], []
        for h in range(2):
            m = head_mask(h, BF)
            s = mm_t(k * m, q) + bias[...]
            w = jnp.exp(s - lse_ref[2 * p + h, :, qr])
            dp = mm_t(v * m, g)
            ds = (w * (dp - delta_ref[2 * p + h, :, qr])).astype(BF)
            dv.append(mm(w.astype(BF), g))
            dk.append(mm(ds, q))
            dq.append(t_mm(ds, k))
        r.dv[p, kr, :] += jnp.where(lane < HD, dv[0], dv[1])
        r.dk[p, kr, :] += jnp.where(lane < HD, dk[0], dk[1])
        r.dq[p, qr, :] += jnp.where(lane < HD, dq[0], dq[1])
        return 0

    lax.fori_loop(0, 4, pair, 0)


def zero_grads(r):
    def step(i, _):
        z = jnp.zeros((4, TILE, 128), F32)
        r.dq[:, rows_of(i), :] = z
        r.dk[:, rows_of(i), :] = z
        r.dv[:, rows_of(i), :] = z
        return 0

    lax.fori_loop(0, 4, step, 0)


def vec(r, row):
    return r.vecs[row : row + 1, :]


def add_vec(r, row, value):
    r.vg[row] += value


def project_self(r, i):
    rows = rows_of(i)
    x = r.tokens[rows, :]
    heads_split(r.q, rows, ((mm(x, r.w[0, :, 0:512]) + vec(r, 0)).astype(BF) * 0.125).astype(BF))
    heads_split(r.k, rows, mm(x, r.w[0, :, 512:1024]).astype(BF))
    heads_split(r.v, rows, (mm(x, r.w[0, :, 1024:1536]) + vec(r, 1)).astype(BF))


def self_bias(r, i, start, count):
    qs = r.tcol[rows_of(i), 0:1]
    ks = r.trow[0:1, start : start + count]
    at = lax.broadcasted_iota(jnp.int32, (TILE, count), 0) + i * TILE
    key = lax.broadcasted_iota(jnp.int32, (TILE, count), 1) + start
    r.bias[:, 0:count] = jnp.where((qs == ks) & (key <= at), 0.0, MASKED)


def after_self(r, i):
    rows = rows_of(i)
    a = heads_join(r.a, rows)
    z = r.tokens[rows, :].astype(F32) + (mm(a, r.w[0, :, 1536:2048]) + vec(r, 2))
    n, inverse = normed(z)
    r.n1[rows, :] = n
    r.r1[rows, :] = jnp.broadcast_to(inverse, (TILE, 128))
    y = (n * vec(r, 3) + vec(r, 4)).astype(BF)
    r.y1[rows, :] = y
    heads_split(r.q2, rows, ((mm(y, r.w[1, :, 0:512]) + vec(r, 5)).astype(BF) * 0.125).astype(BF))


def project_cross(r, i):
    rows = rows_of(i)
    m = r.memory[rows, :]
    heads_split(r.k2, rows, mm(m, r.w[1, :, 512:1024]).astype(BF))
    heads_split(r.v2, rows, (mm(m, r.w[1, :, 1024:1536]) + vec(r, 6)).astype(BF))


def cross_bias(r, i):
    qs = r.tcol[rows_of(i), 0:1]
    ks = r.srow[0:1, :]
    r.bias[...] = jnp.where(qs == ks, 0.0, MASKED)


def middle(r, i):
    rows = rows_of(i)
    y1 = r.n1[rows, :] * vec(r, 3) + vec(r, 4)
    z2 = y1 + (mm(heads_join(r.a2, rows), r.w[1, :, 1536:2048]) + vec(r, 7))
    n2, r2 = normed(z2)
    y2 = n2 * vec(r, 8) + vec(r, 9)
    y2l = y2.astype(BF)
    r.y2[rows, :] = y2l
    f = jnp.zeros((TILE, 512), F32)
    for c in range(4):
        cols = slice(c * 512, (c + 1) * 512)
        u = mm(y2l, r.w[2, :, cols]) + vec(r, 10 + c)
        s = jax.nn.sigmoid(u)
        hd = (u * s).astype(BF)
        r.hd[rows, cols] = hd
        r.gate[:, cols] = s * (1.0 + u * (1.0 - s))
        f = f + mm_t(hd, r.w[3, :, cols])
    n3, r3 = normed(y2 + (f + vec(r, 14)))
    r.layer_out[rows, :] = (n3 * vec(r, 15) + vec(r, 16)).astype(BF)
    g = r.out_grad[rows, :].astype(F32)
    add_vec(r, 15, fold(g * n3))
    add_vec(r, 16, fold(g))
    dz3 = norm_back(g, n3, r3, vec(r, 15))
    df = dz3.astype(BF)
    r.df[rows, :] = df
    add_vec(r, 14, fold(df))
    dy2 = dz3
    for c in range(4):
        cols = slice(c * 512, (c + 1) * 512)
        du = (mm(df, r.w[3, :, cols]) * r.gate[:, cols]).astype(BF)
        r.du[rows, cols] = du
        add_vec(r, 10 + c, fold(du))
        dy2 = dy2 + mm_t(du, r.w[2, :, cols])
    add_vec(r, 8, fold(dy2 * n2))
    add_vec(r, 9, fold(dy2))
    dz2 = norm_back(dy2, n2, r2, vec(r, 8))
    r.dz[rows, :] = dz2
    db = dz2.astype(BF)
    r.db[rows, :] = db
    add_vec(r, 7, fold(db))
    heads_split(r.da, rows, mm_t(db, r.w[1, :, 1536:2048]).astype(BF))
    deltas(r, r.a2, r.da, r.delta, i)


def finish_heads(r, i, scale_rows):
    rows = rows_of(i)
    r.g[rows, 0:512] = (heads_join(r.dq, rows) * 0.125).astype(BF)
    r.g[rows, 512:1024] = heads_join(r.dk, rows).astype(BF)
    r.g[rows, 1024:1536] = heads_join(r.dv, rows).astype(BF)
    add_vec(r, scale_rows, fold(r.g[rows, 0:512]))
    add_vec(r, scale_rows + 1, fold(r.g[rows, 1024:1536]))


def after_cross_back(r, i):
    rows = rows_of(i)
    dq, dk, dv = r.g[rows, 0:512], r.g[rows, 512:1024], r.g[rows, 1024:1536]
    r.memory_grad[rows, :] = mm_t(dk, r.w[1, :, 512:1024]) + mm_t(dv, r.w[1, :, 1024:1536])
    dy1 = r.dz[rows, :] + mm_t(dq, r.w[1, :, 0:512])
    n1 = r.n1[rows, :]
    add_vec(r, 3, fold(dy1 * n1))
    add_vec(r, 4, fold(dy1))
    dz1 = norm_back(dy1, n1, r.r1[rows, 0:1], vec(r, 3))
    r.dz[rows, :] = dz1
    db = dz1.astype(BF)
    r.db[rows, :] = db
    add_vec(r, 2, fold(db))
    heads_split(r.da, rows, mm_t(db, r.w[0, :, 1536:2048]).astype(BF))
    deltas(r, r.a, r.da, r.delta, i)


def after_self_back(r, i):
    rows = rows_of(i)
    dq, dk, dv = r.g[rows, 0:512], r.g[rows, 512:1024], r.g[rows, 1024:1536]
    r.input_grad[rows, :] = r.dz[rows, :] + (
        mm_t(dq, r.w[0, :, 0:512]) + mm_t(dk, r.w[0, :, 512:1024]) + mm_t(dv, r.w[0, :, 1024:1536])
    )


def cross_bias_t(r, i, j):
    ks = r.scol[rows_of(j), 0:1]
    qs = r.trow[0:1, rows_of(i)]
    r.bias_t[...] = jnp.where(ks == qs, 0.0, MASKED)


def self_bias_t(r, i, j):
    ks = r.tcol[rows_of(j), 0:1]
    qs = r.trow[0:1, rows_of(i)]
    key = lax.broadcasted_iota(jnp.int32, (TILE, TILE), 0) + j * TILE
    at = lax.broadcasted_iota(jnp.int32, (TILE, TILE), 1) + i * TILE
    r.bias_t[...] = jnp.where((ks == qs) & (key <= at), 0.0, MASKED)


def loop(n, body):
    def step(i, _):
        body(i)
        return 0

    lax.fori_loop(0, n, step, 0)


def flip(r, source):
    def one(i):
        r.xt[:, rows_of(i)] = source(rows_of(i)).T

    loop(4, one)


def weight_grad(r, chunk_of, count, emit):
    def one(c):
        cols = pl.ds(pl.multiple_of(c * 256, 256), 256)
        emit(c, mm(r.xt[...], chunk_of(cols)))

    loop(count, one)


def run(r, emit, hook=lambda name: None):

    segments(r, r.tlen, r.trow, r.tcol)
    segments(r, r.slen, r.srow, r.scol)

    def clear(i):
        r.vg[i] = jnp.zeros((8, 512), F32)

    loop(24, clear)
    hook("start")
    loop(4, lambda i: project_self(r, i))
    hook("projected")
    for i in range(4):
        start = max(0, i - 2) * TILE
        count = (i + 1) * TILE - start
        self_bias(r, i, start, count)
        attend(r, r.q, r.k, r.v, r.a, r.lse, i, start, count, r.bias)
        hook("self%d" % i)
    loop(4, lambda i: project_cross(r, i))
    loop(4, lambda i: after_self(r, i))
    hook("cross_ready")

    def cross(i):
        cross_bias(r, i)
        attend(r, r.q2, r.k2, r.v2, r.a2, r.lse2, i, 0, 1024, r.bias)

    loop(4, cross)
    hook("crossed")
    loop(4, lambda i: middle(r, i))
    flip(r, lambda rows: r.df[rows, :])
    weight_grad(r, lambda cols: r.hd[:, cols], 8, emit(3, 0))
    flip(r, lambda rows: r.y2[rows, :])
    weight_grad(r, lambda cols: r.du[:, cols], 8, emit(2, 0))
    flip(r, lambda rows: heads_join(r.a2, rows))
    weight_grad(r, lambda cols: r.db[:, cols], 2, emit(1, 6))
    hook("ffn_grads")
    zero_grads(r)

    def cross_back(t):
        i, j = t % 4, t // 4
        cross_bias_t(r, i, j)
        attend_back(r, r.q2, r.k2, r.v2, r.da, r.lse2, r.delta, r.bias_t, i, j)

    loop(16, cross_back)
    loop(4, lambda i: finish_heads(r, i, 5))
    flip(r, lambda rows: r.y1[rows, :])
    weight_grad(r, lambda cols: r.g[:, cols], 2, emit(1, 0))
    flip(r, lambda rows: r.memory[rows, :])
    weight_grad(r, lambda cols: r.g[:, pl.ds(cols.start + 512, 256)], 4, emit(1, 2))
    loop(4, lambda i: after_cross_back(r, i))
    flip(r, lambda rows: heads_join(r.a, rows))
    weight_grad(r, lambda cols: r.db[:, cols], 2, emit(0, 6))
    hook("cross_grads")
    zero_grads(r)

    def self_back_keys(j, _):
        def self_back(i, _):
            self_bias_t(r, i, j)
            attend_back(r, r.q, r.k, r.v, r.da, r.lse, r.delta, r.bias_t, i, j)
            return 0

        return lax.fori_loop(j, jnp.minimum(j + 3, 4), self_back, 0)

    lax.fori_loop(0, 4, self_back_keys, 0)
    loop(4, lambda i: finish_heads(r, i, 0))
    flip(r, lambda rows: r.tokens[rows, :])
    weight_grad(r, lambda cols: r.g[:, cols], 6, emit(0, 0))
    hook("self_grads")
    loop(4, lambda i: after_self_back(r, i))


SCRATCH = [
    ("trow", (8, 1024), jnp.int32), ("tcol", (1024, 128), jnp.int32),
    ("srow", (8, 1024), jnp.int32), ("scol", (1024, 128), jnp.int32),
    ("q", (4, 1024, 128), BF), ("k", (4, 1024, 128), BF), ("v", (4, 1024, 128), BF), ("a", (4, 1024, 128), BF),
    ("q2", (4, 1024, 128), BF), ("k2", (4, 1024, 128), BF), ("v2", (4, 1024, 128), BF), ("a2", (4, 1024, 128), BF),
    ("da", (4, 1024, 128), BF), ("lse", (8, 1, 1024), F32), ("lse2", (8, 1, 1024), F32), ("delta", (8, 1, 1024), F32),
    ("n1", (1024, 512), F32), ("r1", (1024, 128), F32), ("y1", (1024, 512), BF), ("y2", (1024, 512), BF),
    ("hd", (1024, 2048), BF), ("du", (1024, 2048), BF), ("df", (1024, 512), BF), ("db", (1024, 512), BF),
    ("gate", (256, 2048), F32), ("dz", (1024, 512), F32), ("bias", (256, 1024), F32), ("bias_t", (256, 256), F32),
    ("dq", (4, 1024, 128), F32), ("dk", (4, 1024, 128), F32), ("dv", (4, 1024, 128), F32),
    ("xt", (512, 1024), BF), ("vg", (24, 8, 512), F32),
]


def plain_kernel(tlen, slen, tokens, memory, out_grad, w, vecs, layer_out, input_grad, memory_grad, mat_grad, vec_grad, stage, sems, *scratch):
    r = Bag()
    r.tlen, r.slen, r.tokens, r.memory, r.out_grad, r.w, r.vecs = tlen, slen, tokens, memory, out_grad, w, vecs
    r.layer_out, r.input_grad, r.memory_grad = layer_out, input_grad, memory_grad
    for (name, _, _), ref in zip(SCRATCH, scratch):
        setattr(r, name, ref)
    r.g = r.du

    def emit(m, first):
        def one(c, value):
            stage[...] = value
            cp = pltpu.make_async_copy(stage, mat_grad.at[m, :, pl.ds(pl.multiple_of((first + c) * 256, 256), 256)], sems)
            cp.start()
            cp.wait()
        return one

    run(r, emit)
    vec_grad[...] = jnp.sum(r.vg[...], axis=1)


def plain(tlen, slen, tokens, memory, out_grad, w, vecs):
    V = pl.BlockSpec(memory_space=pltpu.VMEM)
    S = pl.BlockSpec(memory_space=pltpu.SMEM)
    return pl.pallas_call(
        plain_kernel,
        out_shape=(
            jax.ShapeDtypeStruct((1024, 512), BF), jax.ShapeDtypeStruct((1024, 512), F32), jax.ShapeDtypeStruct((1024, 512), F32),
            jax.ShapeDtypeStruct((4, 512, 2048), F32), jax.ShapeDtypeStruct((24, 512), F32)),
        in_specs=[S, S, V, V, V, V, V],
        out_specs=(V, V, V, pl.BlockSpec(memory_space=pl.ANY), V),
        scratch_shapes=[pltpu.VMEM((512, 256), F32), pltpu.SemaphoreType.DMA] + [pltpu.VMEM(s, d) for _, s, d in SCRATCH],
        compiler_params=pltpu.CompilerParams(vmem_limit_bytes=63400000),
        name="layer",
    )(tlen, slen, tokens, memory, out_grad, w, vecs)


def adam_update(params, grad_in, moments, factor):
    clipped = factor * grad_in
    first_m = BETA_ONE * moments[0] + (1.0 - BETA_ONE) * clipped
    second_m = BETA_TWO * moments[1] + (1.0 - BETA_TWO) * clipped * clipped
    stepped = first_m / CORRECT_ONE / (jnp.sqrt(second_m / CORRECT_TWO) + ADAM_EPS)
    return (-LEARN_RATE * (stepped + WEIGHT_DECAY * params), first_m, second_m)


def generic_body(tokens, memory, target_lengths, source_lengths, out_grad, weights, vectors, weight_moments, vector_moments):
    axes = ("dp", "shard")
    w = lax.all_gather(weights.astype(BF), axes, axis=1, tiled=True)
    vecs = lax.all_gather(vectors.astype(BF), axes, axis=1, tiled=True).astype(F32)
    vecs = jnp.concatenate([vecs, jnp.zeros((VROWS - vecs.shape[0], vecs.shape[1]), F32)], axis=0)
    layer_out, input_grad, memory_grad, mat_grad, vec_grad = plain(
        target_lengths, source_lengths, tokens, memory, out_grad, w, vecs
    )
    mat_share = lax.psum_scatter(mat_grad, axes, scatter_dimension=1, tiled=True)
    vec_share = lax.psum_scatter(vec_grad[: vectors.shape[0]], axes, scatter_dimension=1, tiled=True)
    squares = jnp.sum(mat_share * mat_share) + jnp.sum(vec_share * vec_share)
    grad_norm = jnp.sqrt(lax.psum(squares, axes))
    factor = jnp.minimum(1.0, CLIP_NORM / (grad_norm + 1e-06))
    weight_steps, weight_first, weight_second = adam_update(weights, mat_share, weight_moments, factor)
    vector_steps, vector_first, vector_second = adam_update(vectors, vec_share, vector_moments, factor)
    return (
        layer_out, input_grad, memory_grad, grad_norm, mat_share, vec_share,
        weight_steps, vector_steps, weight_first, weight_second, vector_first, vector_second,
    )


def solution(mesh):
    both = ("dp", "shard")
    rows, mats, vecs = P(both, None), P(None, both, None), P(None, both)
    return jax.shard_map(
        generic_body,
        mesh=mesh,
        in_specs=(rows, rows, rows, rows, rows, mats, vecs, P(None, None, both, None), P(None, None, both)),
        out_specs=(rows, rows, rows, P(), mats, vecs, mats, vecs, mats, mats, vecs, vecs),
        check_vma=False,
    )
```

time: 1040 us -> 671 us (0.65); the launches traced: 1020 us -> 670 us
  matrix products: 288 us -> 0 us
  Pallas kernels: 0 us -> 204 us
  local copies, waits for them, and re-layouts: 93.2 us -> 4.85 us
  other arithmetic: 89.3 us -> 7.95 us
  blocking collectives: 159 us -> 86.1 us
  loops' own time: 22.7 us -> 0 us
    dot_general x49 -> x0, matrix products: 288 us -> none  [the longest x8 78.9 us: block_scores(): jnp.einsum('qhd,khd->hqk', query_part, key_part, preferred_element_type=j...]
    unnamed x7 -> x4, waiting for transfers between devices: 353 us -> 132 us
    pallas_call x0 -> x1, Pallas kernels: none -> 204 us  [plain(): pl.pallas_call(plain_kernel, out_shape=(jax.ShapeDtypeStruct((1024, 512),...]
    reduce_scatter x0 -> x1, waiting for transfers between devices: none -> 180 us  [generic_body(): lax.psum_scatter(mat_grad, axes, scatter_dimension=1, tiled=True)]
    all_gather x3 -> x1, blocking collectives: 119 us -> 44 us  [generic_body(): lax.all_gather(vectors.astype(BF), axes, axis=1, tiled=True).astype(F32)]
    all_gather x3 -> x1, waiting for transfers between devices: 0.04 us -> 37.1 us  [generic_body(): w = lax.all_gather(weights.astype(BF), axes, axis=1, tiled=True)]
    convert_element_type x9 -> x2, other arithmetic: 34.9 us -> 2.48 us  [the longest x1 1.77 us: generic_body(): w = lax.all_gather(weights.astype(BF), axes, axis=1, tiled=True)]
    reduce_sum x19 -> x2, other arithmetic: 32.4 us -> 2.39 us  [generic_body(): squares = jnp.sum(mat_share * mat_share) + jnp.sum(vec_share * vec_share)]
  transfers between devices with their start and end apart: 5 -> 3, of which waited for: 2 -> 3; matrix products, arithmetic and copies ran while one was open for 15% -> 0% of each run, Pallas kernels for 0% -> 0%
where the time goes in v1:
time: 671 us; the launch traced here: 670 us
  waiting for transfers between devices  350 us (52%)
  Pallas kernels  204 us (30%)
  blocking collectives  86.1 us (13%)
  between operations  17 us (3%)
  other arithmetic  7.95 us (1%)
    pallas_call x1, Pallas kernels, plain(): pl.pallas_call(plain_kernel, out_shape=(jax.ShapeDtypeStruct((1024, 512),...  204 us
    reduce_scatter x1, waiting for transfers between devices, generic_body(): lax.psum_scatter(mat_grad, axes, scatter_dimension=1, tiled=True)  180 us
    unnamed x4, waiting for transfers between devices  132 us
    all_gather x1, blocking collectives, generic_body(): lax.all_gather(vectors.astype(BF), axes, axis=1, tiled=True).astype(F32)  44 us
    psum x1, blocking collectives, generic_body(): grad_norm = jnp.sqrt(lax.psum(squares, axes))  42.1 us
    all_gather x1, waiting for transfers between devices, generic_body(): w = lax.all_gather(weights.astype(BF), axes, axis=1, tiled=True)  37.1 us
  transfers between devices with their start and end apart: 3, of which 3 were waited for; matrix products, arithmetic and copies ran while one was open for 0% of the time, Pallas kernels for 0%

profile of v1, /device:TPU:0, one launch (start us, length us, event | category | flops | bytes accessed | tf_op | source)
XLA Modules:
  0.0 670.4 jit_solution(10391056510321492847)
XLA Ops:
  7.2 0.0 all-gather.2.cloned.1.call-start
  7.2 1.8 convert_element_type.7
  9.0 0.0 all-gather.2.cloned.1.call-update
  9.0 0.0 reduce-scatter.7.cloned.1.call-start
  9.1 0.7 convert_element_type.8
  9.8 44.0 %all_gather.7 = bf16[17,512]{0,1:T(8,128)(2,1)S(1)} all-gather(bf16[17,16]{0,1:T(8,128)(2,1)S(1)} %convert_element_type.8), channel_id=1, replica_groups=mesh['dp'=8,'shard'=4] {'dp','shard'}, dimensions={1}, use_global_device_ids=true | all-gather | bytes 17952 | tf_op jit(solution)/shard_map/all_gather | solution.py:474
  53.8 0.1 copy.29
  53.9 0.6 pad_convert_fusion.vecs
  54.5 37.1 %all-gather.2.cloned.1.call-done.w = bf16[4,512,2048]{2,1,0:T(8,128)(2,1)} async-done(((bf16[4,16,2048]{2,1,0:T(8,128)(2,1)}), bf16[4,512,2048]{2,1,0:T(8,128)(2,1)}) %all-gather.2.cloned.1.call-update) | async-done | bytes 8388624 | tf_op jit(solution)/shard_map/all_gather | solution.py:473
  91.7 204.5 %layer.1 = (bf16[1024,512]{1,0:T(8,128)(2,1)}, f32[1024,512]{1,0:T(8,128)}, f32[1024,512]{1,0:T(8,128)}, f32[4,512,2048]{2,1,0:T(8,128)}, f32[24,512]{1,0:T(8,128)}) custom-call(s32[1,16]{1,0:T(1,128)} %tlen.1, s32[1,16]{1,0:T(1,128)} %slen.1, bf16[1024,512]{1,0:T(8,128)(2,1)} %tokens.1, bf16[1024,512]{1,0:T(8,128)(2,1)} %memory.1, ...), custom_call_target="tpu_custom_call" | custom-call | tf_op jit(solution)/shard_map/layer/pallas_call | solution.py:450
  296.2 1.6 copy.37
  297.8 0.0 reduce-scatter.7.cloned.1.call-update
  297.8 0.0 reduce-scatter.5.cloned.1.call-start
  297.9 0.0 copy-start.2
  297.9 0.0 copy-start.3
  297.9 0.0 copy-start
  297.9 0.0 copy-start.1
  297.9 0.6 reduce-scatter.5.cloned.1.call-update
  298.6 0.0 copy-done.2
  298.6 0.1 copy.32
  298.7 0.0 copy-done.3
  298.7 0.1 copy.39
  298.8 131.7 %reduce-scatter.7.cloned.1.call-done = f32[16,17]{1,0:T(8,128)} async-done(((f32[512,17]{1,0:T(8,128)}), f32[16,17]{1,0:T(8,128)}) %reduce-scatter.7.cloned.1.call-update) | async-done | bytes 1104
  430.4 0.8 copy.38
  431.2 0.6 multiply_reduce_fusion.1
  431.8 180.4 %reduce-scatter.5.cloned.1.call-done = f32[4,16,2048]{2,1,0:T(8,128)} async-done(((f32[4,512,2048]{2,1,0:T(8,128)}), f32[4,16,2048]{2,1,0:T(8,128)}) %reduce-scatter.5.cloned.1.call-update) | async-done | bytes 524304 | tf_op jit(solution)/shard_map/reduce_scatter | solution.py:479
  612.3 1.8 multiply_reduce_fusion
  615.3 0.1 copy.40
  615.4 42.1 %psum.7 = f32[]{:T(128)} all-reduce(f32[]{:T(128)S(6)} %add.44), channel_id=1, replica_groups=mesh['dp'=8,'shard'=4] {'dp','shard'}, use_global_device_ids=true, to_apply=%region_4.0 | all-reduce | flops 1 | bytes 8 | tf_op jit(solution)/shard_map/psum | solution.py:482
  658.3 0.7 copy.34
  659.0 0.7 copy.35
  659.7 0.7 copy.36
  660.3 0.0 copy-done
  660.3 0.0 copy-done.1
  660.3 2.4 add_multiply_fusion
  (2 shorter events, 0.0 us)
Async XLA Ops:
  7.2 84.5 %all-gather.2.cloned.1.call-start = ((), (), s32[]{:S(2)}) async-start(), calls=%async_computation.2 | async-start | bytes 8650752 | tf_op jit(solution)/shard_map/all_gather | solution.py:473
  9.0 421.4 %reduce-scatter.7.cloned.1.call-start = ((), (), s32[]{:S(2)}) async-start(), calls=%async_computation.4 | async-start | bytes 270336
  297.8 314.4 %reduce-scatter.5.cloned.1.call-start = ((), (), s32[]{:S(2)}) async-start(), calls=%async_computation.3 | async-start | bytes 17301504 | tf_op jit(solution)/shard_map/reduce_scatter | solution.py:479
  297.9 0.7 copy-start.2
  297.9 0.8 copy-start.3
  297.9 362.4 %copy-start = (f32[4,16,2048]{2,1,0:T(8,128)S(1)}, f32[4,16,2048]{2,1,0:T(8,128)}, u32[]{:S(2)}) copy-start(f32[4,16,2048]{2,1,0:T(8,128)} %param.14) | copy-start | bytes 1572868
  297.9 362.4 %copy-start.1 = (f32[2,4,16,2048]{3,2,1,0:T(8,128)S(1)}, f32[2,4,16,2048]{3,2,1,0:T(8,128)}, u32[]{:S(2)}) copy-start(f32[2,4,16,2048]{3,2,1,0:T(8,128)} %param.16) | copy-start | bytes 3145732
Sparse Core Ops, SparseCore 0:
  11.5 80.1 all-gather.1
  297.9 132.4 reduce-scatter.6
  433.4 178.8 reduce-scatter.4

commit v2 on v1

--- a/solution.py
+++ b/solution.py
@@ -13,6 +13,7 @@
 F32 = jnp.float32
 TILE = 256
 VROWS = 24
+MESH = pl.DeviceIdType.MESH
 CLIP_NORM = 1.0
 LEARN_RATE = 0.001
 BETA_ONE = 0.9
@@ -77,27 +78,25 @@
     return jnp.where((lane < HD) if h == 0 else (lane >= HD), 1.0, 0.0).astype(dtype)
 
 
-def segments(r, lengths, row_ref, col_ref):
+def segments(r, lengths, row_ref, lane):
     ends = []
     total = jnp.int32(0)
     for s in range(16):
         total = total + lengths[0, s]
         ends.append(total)
-    place = lax.broadcasted_iota(jnp.int32, (8, 1024), 1)
-    seg = jnp.zeros((8, 1024), jnp.int32)
-    for e in ends:
-        seg = seg + jnp.where(e <= place, 1, 0)
-    row_ref[...] = seg
-
-    def col(i, _):
-        at = lax.broadcasted_iota(jnp.int32, (TILE, 128), 0) + i * TILE
-        c = jnp.zeros((TILE, 128), jnp.int32)
+
+    def number(at):
+        seg = jnp.zeros(at.shape, F32)
         for e in ends:
-            c = c + jnp.where(e <= at, 1, 0)
-        col_ref[rows_of(i), :] = c
-        return 0
-
-    lax.fori_loop(0, 4, col, 0)
+            seg = seg + jnp.where(e <= at, 1.0, 0.0)
+        return seg
+
+    row_ref[...] = number(lax.broadcasted_iota(jnp.int32, (8, 1024), 1))
+
+    def col(i):
+        r.cols[rows_of(i), lane : lane + 1] = number(lax.broadcasted_iota(jnp.int32, (TILE, 128), 0) + i * TILE)[:, 0:1]
+
+    loop(4, col)
 
 
 def attend(r, q_ref, k_ref, v_ref, out_ref, lse_ref, tile, key_start, key_count, bias):
@@ -186,13 +185,13 @@
 def project_self(r, i):
     rows = rows_of(i)
     x = r.tokens[rows, :]
-    heads_split(r.q, rows, ((mm(x, r.w[0, :, 0:512]) + vec(r, 0)).astype(BF) * 0.125).astype(BF))
-    heads_split(r.k, rows, mm(x, r.w[0, :, 512:1024]).astype(BF))
-    heads_split(r.v, rows, (mm(x, r.w[0, :, 1024:1536]) + vec(r, 1)).astype(BF))
+    heads_split(r.q, rows, ((mm(x, r.w(0, 0, 512)) + vec(r, 0)).astype(BF) * 0.125).astype(BF))
+    heads_split(r.k, rows, mm(x, r.w(0, 512, 1024)).astype(BF))
+    heads_split(r.v, rows, (mm(x, r.w(0, 1024, 1536)) + vec(r, 1)).astype(BF))
 
 
 def self_bias(r, i, start, count):
-    qs = r.tcol[rows_of(i), 0:1]
+    qs = r.cols[rows_of(i), 0:1]
     ks = r.trow[0:1, start : start + count]
     at = lax.broadcasted_iota(jnp.int32, (TILE, count), 0) + i * TILE
     key = lax.broadcasted_iota(jnp.int32, (TILE, count), 1) + start
@@ -202,24 +201,24 @@
 def after_self(r, i):
     rows = rows_of(i)
     a = heads_join(r.a, rows)
-    z = r.tokens[rows, :].astype(F32) + (mm(a, r.w[0, :, 1536:2048]) + vec(r, 2))
+    z = r.tokens[rows, :].astype(F32) + (mm(a, r.w(0, 1536, 2048)) + vec(r, 2))
     n, inverse = normed(z)
     r.n1[rows, :] = n
-    r.r1[rows, :] = jnp.broadcast_to(inverse, (TILE, 128))
+    r.cols[rows, 2:3] = inverse
     y = (n * vec(r, 3) + vec(r, 4)).astype(BF)
     r.y1[rows, :] = y
-    heads_split(r.q2, rows, ((mm(y, r.w[1, :, 0:512]) + vec(r, 5)).astype(BF) * 0.125).astype(BF))
+    heads_split(r.q2, rows, ((mm(y, r.w(1, 0, 512)) + vec(r, 5)).astype(BF) * 0.125).astype(BF))
 
 
 def project_cross(r, i):
     rows = rows_of(i)
     m = r.memory[rows, :]
-    heads_split(r.k2, rows, mm(m, r.w[1, :, 512:1024]).astype(BF))
-    heads_split(r.v2, rows, (mm(m, r.w[1, :, 1024:1536]) + vec(r, 6)).astype(BF))
+    heads_split(r.k2, rows, mm(m, r.w(1, 512, 1024)).astype(BF))
+    heads_split(r.v2, rows, (mm(m, r.w(1, 1024, 1536)) + vec(r, 6)).astype(BF))
 
 
 def cross_bias(r, i):
-    qs = r.tcol[rows_of(i), 0:1]
+    qs = r.cols[rows_of(i), 0:1]
     ks = r.srow[0:1, :]
     r.bias[...] = jnp.where(qs == ks, 0.0, MASKED)
 
@@ -227,7 +226,7 @@
 def middle(r, i):
     rows = rows_of(i)
     y1 = r.n1[rows, :] * vec(r, 3) + vec(r, 4)
-    z2 = y1 + (mm(heads_join(r.a2, rows), r.w[1, :, 1536:2048]) + vec(r, 7))
+    z2 = y1 + (mm(heads_join(r.a2, rows), r.w(1, 1536, 2048)) + vec(r, 7))
     n2, r2 = normed(z2)
     y2 = n2 * vec(r, 8) + vec(r, 9)
     y2l = y2.astype(BF)
@@ -235,15 +234,15 @@
     f = jnp.zeros((TILE, 512), F32)
     for c in range(4):
         cols = slice(c * 512, (c + 1) * 512)
-        u = mm(y2l, r.w[2, :, cols]) + vec(r, 10 + c)
+        u = mm(y2l, r.w(2, cols.start, cols.stop)) + vec(r, 10 + c)
         s = jax.nn.sigmoid(u)
         hd = (u * s).astype(BF)
-        r.hd[rows, cols] = hd
+        r.put_hidden(i, cols, hd)
         r.gate[:, cols] = s * (1.0 + u * (1.0 - s))
-        f = f + mm_t(hd, r.w[3, :, cols])
+        f = f + mm_t(hd, r.w(3, cols.start, cols.stop))
     n3, r3 = normed(y2 + (f + vec(r, 14)))
-    r.layer_out[rows, :] = (n3 * vec(r, 15) + vec(r, 16)).astype(BF)
-    g = r.out_grad[rows, :].astype(F32)
+    r.put_layer_out(i, (n3 * vec(r, 15) + vec(r, 16)).astype(BF))
+    g = r.get_out_grad(i).astype(F32)
     add_vec(r, 15, fold(g * n3))
     add_vec(r, 16, fold(g))
     dz3 = norm_back(g, n3, r3, vec(r, 15))
@@ -253,10 +252,10 @@
     dy2 = dz3
     for c in range(4):
         cols = slice(c * 512, (c + 1) * 512)
-        du = (mm(df, r.w[3, :, cols]) * r.gate[:, cols]).astype(BF)
+        du = (mm(df, r.w(3, cols.start, cols.stop)) * r.gate[:, cols]).astype(BF)
         r.du[rows, cols] = du
         add_vec(r, 10 + c, fold(du))
-        dy2 = dy2 + mm_t(du, r.w[2, :, cols])
+        dy2 = dy2 + mm_t(du, r.w(2, cols.start, cols.stop))
     add_vec(r, 8, fold(dy2 * n2))
     add_vec(r, 9, fold(dy2))
     dz2 = norm_back(dy2, n2, r2, vec(r, 8))
@@ -264,7 +263,7 @@
     db = dz2.astype(BF)
     r.db[rows, :] = db
     add_vec(r, 7, fold(db))
-    heads_split(r.da, rows, mm_t(db, r.w[1, :, 1536:2048]).astype(BF))
+    heads_split(r.da, rows, mm_t(db, r.w(1, 1536, 2048)).astype(BF))
     deltas(r, r.a2, r.da, r.delta, i)
 
 
@@ -280,40 +279,42 @@
 def after_cross_back(r, i):
     rows = rows_of(i)
     dq, dk, dv = r.g[rows, 0:512], r.g[rows, 512:1024], r.g[rows, 1024:1536]
-    r.memory_grad[rows, :] = mm_t(dk, r.w[1, :, 512:1024]) + mm_t(dv, r.w[1, :, 1024:1536])
-    dy1 = r.dz[rows, :] + mm_t(dq, r.w[1, :, 0:512])
+    r.put_memory_grad(i, mm_t(dk, r.w(1, 512, 1024)) + mm_t(dv, r.w(1, 1024, 1536)))
+    dy1 = r.dz[rows, :] + mm_t(dq, r.w(1, 0, 512))
     n1 = r.n1[rows, :]
     add_vec(r, 3, fold(dy1 * n1))
     add_vec(r, 4, fold(dy1))
-    dz1 = norm_back(dy1, n1, r.r1[rows, 0:1], vec(r, 3))
+    dz1 = norm_back(dy1, n1, r.cols[rows, 2:3], vec(r, 3))
     r.dz[rows, :] = dz1
     db = dz1.astype(BF)
     r.db[rows, :] = db
     add_vec(r, 2, fold(db))
-    heads_split(r.da, rows, mm_t(db, r.w[0, :, 1536:2048]).astype(BF))
+    heads_split(r.da, rows, mm_t(db, r.w(0, 1536, 2048)).astype(BF))
     deltas(r, r.a, r.da, r.delta, i)
 
 
 def after_self_back(r, i):
     rows = rows_of(i)
     dq, dk, dv = r.g[rows, 0:512], r.g[rows, 512:1024], r.g[rows, 1024:1536]
-    r.input_grad[rows, :] = r.dz[rows, :] + (
-        mm_t(dq, r.w[0, :, 0:512]) + mm_t(dk, r.w[0, :, 512:1024]) + mm_t(dv, r.w[0, :, 1024:1536])
+    r.put_input_grad(
+        i,
+        r.dz[rows, :]
+        + (mm_t(dq, r.w(0, 0, 512)) + mm_t(dk, r.w(0, 512, 1024)) + mm_t(dv, r.w(0, 1024, 1536))),
     )
 
 
 def cross_bias_t(r, i, j):
-    ks = r.scol[rows_of(j), 0:1]
+    ks = r.cols[rows_of(j), 1:2]
     qs = r.trow[0:1, rows_of(i)]
-    r.bias_t[...] = jnp.where(ks == qs, 0.0, MASKED)
+    r.bias[:, 0:TILE] = jnp.where(ks == qs, 0.0, MASKED)
 
 
 def self_bias_t(r, i, j):
-    ks = r.tcol[rows_of(j), 0:1]
+    ks = r.cols[rows_of(j), 0:1]
     qs = r.trow[0:1, rows_of(i)]
     key = lax.broadcasted_iota(jnp.int32, (TILE, TILE), 0) + j * TILE
     at = lax.broadcasted_iota(jnp.int32, (TILE, TILE), 1) + i * TILE
-    r.bias_t[...] = jnp.where((ks == qs) & (key <= at), 0.0, MASKED)
+    r.bias[:, 0:TILE] = jnp.where((ks == qs) & (key <= at), 0.0, MASKED)
 
 
 def loop(n, body):
@@ -339,15 +340,14 @@
     loop(count, one)
 
 
-def run(r, emit, hook=lambda name: None):
-
-    segments(r, r.tlen, r.trow, r.tcol)
-    segments(r, r.slen, r.srow, r.scol)
+def run(r, emit, hook=lambda name: None, at_step=lambda name, t: None):
+    segments(r, r.tlen, r.trow, 0)
+    segments(r, r.slen, r.srow, 1)
 
     def clear(i):
         r.vg[i] = jnp.zeros((8, 512), F32)
 
-    loop(24, clear)
+    loop(VROWS, clear)
     hook("start")
     loop(4, lambda i: project_self(r, i))
     hook("projected")
@@ -364,23 +364,28 @@
     def cross(i):
         cross_bias(r, i)
         attend(r, r.q2, r.k2, r.v2, r.a2, r.lse2, i, 0, 1024, r.bias)
+        at_step("cross", i)
 
     loop(4, cross)
     hook("crossed")
     loop(4, lambda i: middle(r, i))
+    hook("middle")
     flip(r, lambda rows: r.df[rows, :])
-    weight_grad(r, lambda cols: r.hd[:, cols], 8, emit(3, 0))
+    weight_grad(r, r.get_hidden, 8, emit(3, 0))
+    hook("grads3")
     flip(r, lambda rows: r.y2[rows, :])
     weight_grad(r, lambda cols: r.du[:, cols], 8, emit(2, 0))
+    hook("grads2")
     flip(r, lambda rows: heads_join(r.a2, rows))
     weight_grad(r, lambda cols: r.db[:, cols], 2, emit(1, 6))
-    hook("ffn_grads")
+    hook("grads1o")
     zero_grads(r)
 
     def cross_back(t):
         i, j = t % 4, t // 4
         cross_bias_t(r, i, j)
-        attend_back(r, r.q2, r.k2, r.v2, r.da, r.lse2, r.delta, r.bias_t, i, j)
+        attend_back(r, r.q2, r.k2, r.v2, r.da, r.lse2, r.delta, r.bias.at[:, 0:TILE], i, j)
+        at_step("cross_back", t)
 
     loop(16, cross_back)
     loop(4, lambda i: finish_heads(r, i, 5))
@@ -388,56 +393,78 @@
     weight_grad(r, lambda cols: r.g[:, cols], 2, emit(1, 0))
     flip(r, lambda rows: r.memory[rows, :])
     weight_grad(r, lambda cols: r.g[:, pl.ds(cols.start + 512, 256)], 4, emit(1, 2))
+    hook("grads1")
     loop(4, lambda i: after_cross_back(r, i))
     flip(r, lambda rows: heads_join(r.a, rows))
     weight_grad(r, lambda cols: r.db[:, cols], 2, emit(0, 6))
-    hook("cross_grads")
+    hook("grads0o")
     zero_grads(r)
-
-    def self_back_keys(j, _):
-        def self_back(i, _):
-            self_bias_t(r, i, j)
-            attend_back(r, r.q, r.k, r.v, r.da, r.lse, r.delta, r.bias_t, i, j)
-            return 0
-
-        return lax.fori_loop(j, jnp.minimum(j + 3, 4), self_back, 0)
-
-    lax.fori_loop(0, 4, self_back_keys, 0)
+    for gap in range(3):
+
+        def self_back(j):
+            self_bias_t(r, j + gap, j)
+            attend_back(r, r.q, r.k, r.v, r.da, r.lse, r.delta, r.bias.at[:, 0:TILE], j + gap, j)
+            at_step("self_back%d" % gap, j)
+
+        loop(4 - gap, self_back)
     loop(4, lambda i: finish_heads(r, i, 0))
     flip(r, lambda rows: r.tokens[rows, :])
     weight_grad(r, lambda cols: r.g[:, cols], 6, emit(0, 0))
-    hook("self_grads")
+    hook("grads0")
     loop(4, lambda i: after_self_back(r, i))
 
 
 SCRATCH = [
-    ("trow", (8, 1024), jnp.int32), ("tcol", (1024, 128), jnp.int32),
-    ("srow", (8, 1024), jnp.int32), ("scol", (1024, 128), jnp.int32),
+    ("trow", (8, 1024), F32), ("srow", (8, 1024), F32), ("cols", (1024, 128), F32),
     ("q", (4, 1024, 128), BF), ("k", (4, 1024, 128), BF), ("v", (4, 1024, 128), BF), ("a", (4, 1024, 128), BF),
     ("q2", (4, 1024, 128), BF), ("k2", (4, 1024, 128), BF), ("v2", (4, 1024, 128), BF), ("a2", (4, 1024, 128), BF),
     ("da", (4, 1024, 128), BF), ("lse", (8, 1, 1024), F32), ("lse2", (8, 1, 1024), F32), ("delta", (8, 1, 1024), F32),
-    ("n1", (1024, 512), F32), ("r1", (1024, 128), F32), ("y1", (1024, 512), BF), ("y2", (1024, 512), BF),
-    ("hd", (1024, 2048), BF), ("du", (1024, 2048), BF), ("df", (1024, 512), BF), ("db", (1024, 512), BF),
-    ("gate", (256, 2048), F32), ("dz", (1024, 512), F32), ("bias", (256, 1024), F32), ("bias_t", (256, 256), F32),
+    ("n1", (1024, 512), F32), ("y1", (1024, 512), BF), ("y2", (1024, 512), BF),
+    ("hd", (2, 2, 4, 2, 2, 16, 2048), BF), ("du", (1024, 2048), BF), ("df", (1024, 512), BF), ("db", (1024, 512), BF),
+    ("gate", (256, 2048), F32), ("dz", (1024, 512), F32), ("bias", (256, 1024), F32),
     ("dq", (4, 1024, 128), F32), ("dk", (4, 1024, 128), F32), ("dv", (4, 1024, 128), F32),
     ("xt", (512, 1024), BF), ("vg", (24, 8, 512), F32),
 ]
 
 
-def plain_kernel(tlen, slen, tokens, memory, out_grad, w, vecs, layer_out, input_grad, memory_grad, mat_grad, vec_grad, stage, sems, *scratch):
+def hidden_access(r):
+    def put(i, cols, value):
+        r.hd[i // 2, i % 2, :, :, :, :, cols] = value.reshape(4, 2, 2, 16, 512)
+
+    def get(cols):
+        return r.hd[:, :, :, :, :, :, cols].reshape(1024, 256)
+
+    r.put_hidden, r.get_hidden = put, get
+
+
+def plain_kernel(
+    tlen, slen, tokens, memory, out_grad, w, vecs, layer_out, input_grad, memory_grad, mat_grad, vec_grad, stage, sem, *scratch
+):
     r = Bag()
-    r.tlen, r.slen, r.tokens, r.memory, r.out_grad, r.w, r.vecs = tlen, slen, tokens, memory, out_grad, w, vecs
-    r.layer_out, r.input_grad, r.memory_grad = layer_out, input_grad, memory_grad
+    r.tlen, r.slen, r.tokens, r.memory, r.vecs = tlen, slen, tokens, memory, vecs
     for (name, _, _), ref in zip(SCRATCH, scratch):
         setattr(r, name, ref)
     r.g = r.du
+    r.w = lambda m, a, b: w[m, :, a:b]
+    hidden_access(r)
+    r.get_out_grad = lambda i: out_grad[rows_of(i), :]
+
+    def put_to(ref):
+        def put(i, value):
+            ref[rows_of(i), :] = value
+
+        return put
+
+    r.put_layer_out, r.put_memory_grad, r.put_input_grad = put_to(layer_out), put_to(memory_grad), put_to(input_grad)
 
     def emit(m, first):
         def one(c, value):
             stage[...] = value
-            cp = pltpu.make_async_copy(stage, mat_grad.at[m, :, pl.ds(pl.multiple_of((first + c) * 256, 256), 256)], sems)
-            cp.start()
-            cp.wait()
+            cols = pl.ds(pl.multiple_of((first + c) * 256, 256), 256)
+            copy = pltpu.make_async_copy(stage, mat_grad.at[m, :, cols], sem)
+            copy.start()
+            copy.wait()
+
         return one
 
     run(r, emit)
@@ -450,14 +477,526 @@
     return pl.pallas_call(
         plain_kernel,
         out_shape=(
-            jax.ShapeDtypeStruct((1024, 512), BF), jax.ShapeDtypeStruct((1024, 512), F32), jax.ShapeDtypeStruct((1024, 512), F32),
-            jax.ShapeDtypeStruct((4, 512, 2048), F32), jax.ShapeDtypeStruct((24, 512), F32)),
+            jax.ShapeDtypeStruct((1024, 512), BF),
+            jax.ShapeDtypeStruct((1024, 512), F32),
+            jax.ShapeDtypeStruct((1024, 512), F32),
+            jax.ShapeDtypeStruct((4, 512, 2048), F32),
+            jax.ShapeDtypeStruct((VROWS, 512), F32),
+        ),
         in_specs=[S, S, V, V, V, V, V],
         out_specs=(V, V, V, pl.BlockSpec(memory_space=pl.ANY), V),
         scratch_shapes=[pltpu.VMEM((512, 256), F32), pltpu.SemaphoreType.DMA] + [pltpu.VMEM(s, d) for _, s, d in SCRATCH],
         compiler_params=pltpu.CompilerParams(vmem_limit_bytes=63400000),
         name="layer",
     )(tlen, slen, tokens, memory, out_grad, w, vecs)
+
+
+class Place:
+    def __init__(self):
+        dp, sh = lax.axis_index("dp"), lax.axis_index("shard")
+        self.z, self.y, self.x, self.c = dp // 2, dp % 2, sh // 2, sh % 2
+        z, y, x, c = self.z, self.y, self.x, self.c
+        self.y1, self.x1 = y + c * (1 - 2 * y), x + (1 - c) * (1 - 2 * x)
+        self.y2, self.x2 = y + (1 - c) * (1 - 2 * y), x + c * (1 - 2 * x)
+        self.y3, self.x3 = 1 - y, 1 - x
+        self.i1, self.i2 = x * (1 - c) + y * c, y * (1 - c) + x * c
+        self.first = (z * 2 + self.y1, self.x1 * 2 + c)
+        self.second = (z * 2 + self.y2, self.x2 * 2 + c)
+        self.twin = (z * 2 + y, x * 2 + 1 - c)
+
+    def along_z(self, d):
+        return (lax.rem(self.z + d, 4) * 2 + self.y, self.x * 2 + self.c)
+
+    def in_plane(self, n):
+        flat = lax.rem(self.y * 4 + self.x * 2 + self.c + n, 8)
+        return (self.z * 2 + flat // 4, flat % 4)
+
+
+class Gather:
+    def __init__(self, at, ref, cols, index, send, recv):
+        self.at, self.ref, self.cols, self.index, self.send, self.recv = at, ref, cols, index, send, recv
+        self.started = []
+
+    def column(self, y, x, c):
+        return self.ref.at[:, y, x, c, :, self.cols]
+
+    def copy(self, slot, what, device):
+        return pltpu.make_async_remote_copy(
+            src_ref=what,
+            dst_ref=what,
+            send_sem=self.send.at[self.index, slot],
+            recv_sem=self.recv.at[self.index, slot],
+            device_id=device,
+            device_id_type=MESH,
+        )
+
+    def go(self, slot, what, device):
+        copy = self.copy(slot, what, device)
+        copy.start()
+        self.started.append(copy)
+
+    def step0(self):
+        p = self.at
+        for d in range(1, 4):
+            self.go(d - 1, self.ref.at[p.z, p.y, p.x, p.c, :, self.cols], p.along_z(d))
+
+    def step1(self):
+        p = self.at
+        for d in range(1, 4):
+            self.copy(d - 1, self.ref.at[lax.rem(p.z + 4 - d, 4), p.y, p.x, p.c, :, self.cols], p.along_z(d)).wait_recv()
+        own = self.column(p.y, p.x, p.c)
+        self.go(3, own, p.second)
+        self.go(4, own, p.first)
+        self.go(5, own, p.twin)
+
+    def step2(self):
+        p = self.at
+        got = self.column(p.y2, p.x2, p.c)
+        self.copy(3, got, p.second).wait_recv()
+        self.go(6, got, p.first)
+        self.go(7, got, p.twin)
+
+    def step3(self):
+        p = self.at
+        got = self.column(p.y1, p.x1, p.c)
+        self.copy(4, got, p.first).wait_recv()
+        self.go(8, got, p.twin)
+        far = self.column(p.y3, p.x3, p.c)
+        self.copy(6, far, p.first).wait_recv()
+        self.go(9, far, p.twin)
+
+    def step4(self):
+        p = self.at
+        for slot, y, x in ((5, p.y, p.x), (7, p.y1, p.x1), (8, p.y2, p.x2), (9, p.y3, p.x3)):
+            self.copy(slot, self.column(y, x, 1 - p.c), p.twin).wait_recv()
+
+    def finish(self):
+        for copy in self.started:
+            copy.wait_send()
+        self.started = []
+
+
+class Reduce:
+    def __init__(self, at, keep, give, recvs, own, cols, index, send, recv):
+        self.at, self.keep, self.give, self.recvs, self.own, self.cols = at, keep, give, recvs, own, cols
+        self.index, self.send, self.recv = index, send, recv
+
+    def copy(self, slot):
+        p, cols = self.at, self.cols
+        if slot == 0:
+            what, where, device = self.give.at[:, :, :, :, cols], self.recvs[0].at[:, :, :, :, cols], p.twin
+        elif slot == 1:
+            what, where, device = self.keep.at[:, :, 1 - p.i1, :, cols], self.recvs[1].at[:, :, :, cols], p.first
+        elif slot == 2:
+            what, where, device = self.keep.at[:, 1 - p.i2, p.i1, :, cols], self.recvs[2].at[:, :, cols], p.second
+        else:
+            d = slot - 2
+            what = self.keep.at[lax.rem(p.z + d, 4), p.i2, p.i1, :, cols]
+            where, device = self.recvs[3].at[d - 1, :, cols], p.along_z(d)
+        return pltpu.make_async_remote_copy(
+            src_ref=what,
+            dst_ref=where,
+            send_sem=self.send.at[self.index, slot],
+            recv_sem=self.recv.at[self.index, slot],
+            device_id=device,
+            device_id_type=MESH,
+        )
+
+    def step0(self):
+        self.copy(0).start()
+
+    def step1(self):
+        cols = self.cols
+        self.copy(0).wait_recv()
+
+        def add(z):
+            self.keep[z, :, :, :, cols] = (
+                self.keep[z, :, :, :, cols].astype(F32) + self.recvs[0][z, :, :, :, cols].astype(F32)
+            ).astype(BF)
+
+        loop(4, add)
+        self.copy(1).start()
+
+    def step2(self):
+        p, cols = self.at, self.cols
+        self.copy(1).wait_recv()
+        self.keep[:, :, p.i1, :, cols] = (
+            self.keep[:, :, p.i1, :, cols].astype(F32) + self.recvs[1][:, :, :, cols].astype(F32)
+        ).astype(BF)
+        self.copy(2).start()
+
+    def step3(self):
+        p, cols = self.at, self.cols
+        self.copy(2).wait_recv()
+        self.keep[:, p.i2, p.i1, :, cols] = (
+            self.keep[:, p.i2, p.i1, :, cols].astype(F32) + self.recvs[2][:, :, cols].astype(F32)
+        ).astype(BF)
+        for slot in range(3, 6):
+            self.copy(slot).start()
+
+    def step4(self):
+        p, cols = self.at, self.cols
+        total = self.keep[p.z, p.i2, p.i1, :, cols].astype(F32)
+        for slot in range(3, 6):
+            self.copy(slot).wait_recv()
+            total = total + self.recvs[3][slot - 3, :, cols].astype(F32)
+        self.own[:, cols] = total
+
+    def finish(self):
+        for slot in range(6):
+            self.copy(slot).wait_send()
+
+
+def steps_of(jobs, names=("step0", "step1", "step2", "step3", "step4"), ready=None):
+    ticks = []
+    for t in range(len(jobs) + len(names) - 1):
+        tick = []
+        for s in range(len(names)):
+            k = t - s
+            if 0 <= k < len(jobs):
+                tick.append(getattr(jobs[k], names[s]))
+        ticks.append(tick)
+    return ticks
+
+
+FUSED_SCRATCH = [
+    ("g0", (4, 2, 2, 2, 16, 2176), BF),
+    ("g1", (4, 2, 2, 2, 16, 2048), BF),
+    ("g2", (4, 2, 2, 2, 16, 2048), BF),
+    ("g3", (4, 2, 2, 2, 16, 2048), BF),
+    ("own", (64, 2048), F32),
+    ("square", (128, 128), F32),
+    ("vecs", (VROWS, 512), F32),
+    ("ra", (4, 4, 2, 2, 16, 2048), BF),
+    ("rb", (4, 4, 2, 16, 2048), BF),
+    ("rc", (4, 4, 16, 2048), BF),
+    ("rd", (4, 3, 16, 2048), BF),
+    ("vkeep", (4, 2, 2, 16, 128), BF),
+    ("vgive", (4, 2, 2, 16, 128), BF),
+    ("va", (4, 2, 2, 16, 128), BF),
+    ("vb", (4, 2, 16, 128), BF),
+    ("vc", (4, 16, 128), BF),
+    ("vd", (3, 16, 128), BF),
+    ("vown", (16, 128), F32),
+    ("nsend", (2, 8, 128), F32),
+    ("nrecv", (10, 8, 128), F32),
+]
+N_GATHER = 12
+N_REDUCE = 7
+
+
+def adam_parts(params, grad_in, first, second, factor):
+    clipped = factor * grad_in
+    first_m = BETA_ONE * first + (1.0 - BETA_ONE) * clipped
+    second_m = BETA_TWO * second + (1.0 - BETA_TWO) * clipped * clipped
+    stepped = first_m / CORRECT_ONE / (jnp.sqrt(second_m / CORRECT_TWO) + ADAM_EPS)
+    return (-LEARN_RATE * (stepped + WEIGHT_DECAY * params), first_m, second_m)
+
+
+def fused_kernel(
+    tlen, slen, tokens, memory, out_grad, weights, vectors, moments, vector_moments,
+    layer_out, input_grad, memory_grad, norm_out, mat_out, vec_out, step_out, vstep_out, first_out, second_out, vfirst_out, vsecond_out,
+    *scratch,
+):
+    r = Bag()
+    names = [n for n, _, _ in SCRATCH] + [n for n, _, _ in FUSED_SCRATCH]
+    for name, ref in zip(names, scratch):
+        setattr(r, name, ref)
+    g_send, g_recv, s_send, s_recv, n_send, n_recv, l_sem = scratch[len(names) :]
+    p = Place()
+    r.tlen, r.slen, r.tokens, r.memory = tlen, slen, tokens, memory
+    r.g = r.du
+    hidden_access(r)
+    mats = [r.g0, r.g1, r.g2, r.g3]
+
+    def w(m, a, b):
+        shift = 128 if m == 0 else 0
+        return mats[m][:, :, :, :, :, a + shift : b + shift].reshape(512, b - a)
+
+    r.w = w
+
+    barrier = pltpu.get_barrier_semaphore()
+    for d in range(1, 4):
+        pl.semaphore_signal(barrier, inc=1, device_id=p.along_z(d), device_id_type=MESH)
+    for n in range(1, 8):
+        pl.semaphore_signal(barrier, inc=1, device_id=p.in_plane(n), device_id_type=MESH)
+
+    local = []
+
+    def fetch(k, src, dst):
+        copy = pltpu.make_async_copy(src, dst, l_sem.at[k])
+        copy.start()
+        local.append(copy)
+        return copy
+
+    weights_in = fetch(0, weights, r.gate.at[128:192, :])
+    grad_in = fetch(1, out_grad, r.db)
+    r.square[...] = jnp.zeros((128, 128), F32)
+    r.square[0:17, 0:16] = vectors[...]
+    r.g0[p.z, p.y, p.x, p.c, :, 0:128] = r.square[...].T[0:16, :].astype(BF)
+    weights_in.wait()
+    for m in range(4):
+        shift = 128 if m == 0 else 0
+        mats[m][p.z, p.y, p.x, p.c, :, shift : shift + 2048] = r.gate[128 + 16 * m : 144 + 16 * m, :].astype(BF)
+    pl.semaphore_wait(barrier, 10)
+
+    gathers = []
+    for m, cuts in ((0, (0, 640, 1152, 1664, 2176)), (1, (0, 512, 1024, 1536, 2048)), (2, (0, 1024, 2048)), (3, (0, 1024, 2048))):
+        for a, b in zip(cuts[:-1], cuts[1:]):
+            gathers.append(Gather(p, mats[m], slice(a, b), len(gathers), g_send, g_recv))
+    ticks = steps_of(gathers)
+
+    def run_ticks(n):
+        for _ in range(n):
+            if ticks:
+                for action in ticks.pop(0):
+                    action()
+
+    keeps = {0: r.hd.at[1, 0], 1: r.hd.at[0, 0], 2: r.g2.at[:, :, :, 0], 3: r.g3.at[:, :, :, 0]}
+    gives = {0: r.hd.at[1, 1], 1: r.hd.at[0, 1], 2: r.g2.at[:, :, :, 1], 3: r.g3.at[:, :, :, 1]}
+
+    def spread(value, keep, give, cols):
+        v = value.reshape(4, 2, 2, 2, 16, value.shape[-1])
+        flag = p.c == 0
+        for y in range(2):
+            for x in range(2):
+                i1, i2 = x * (1 - p.c) + y * p.c, y * (1 - p.c) + x * p.c
+                even, odd = v[:, y, x, 0], v[:, y, x, 1]
+                keep[:, i2, i1, :, cols] = jnp.where(flag, even, odd).astype(BF)
+                give[:, i1, i2, :, cols] = jnp.where(flag, odd, even).astype(BF)
+
+    def emit(m, first):
+        def one(c, value):
+            spread(value, keeps[m], gives[m], pl.ds(pl.multiple_of((first + c) * 256, 256), 256))
+
+        return one
+
+    def job(k, m, a, b):
+        return Reduce(
+            p, keeps[m], gives[m], (r.ra.at[m], r.rb.at[m], r.rc.at[m], r.rd.at[m]),
+            r.own.at[16 * m : 16 * m + 16, :], slice(a, b), k, s_send, s_recv,
+        )
+
+    j3, j2, j1o, j1, j0o, j0 = (
+        job(0, 3, 0, 2048), job(1, 2, 0, 2048), job(2, 1, 1536, 2048), job(3, 1, 0, 1536), job(4, 0, 1536, 2048), job(5, 0, 0, 1536),
+    )
+    jv = Reduce(p, r.vkeep, r.vgive, (r.va, r.vb, r.vc, r.vd), r.vown, slice(0, 128), 6, s_send, s_recv)
+    jobs = [j3, j2, j1o, j1, j0o, j0, jv]
+
+    def hook(name):
+        if name == "start":
+            run_ticks(5)
+            for b in range(4):
+                block = r.g0[b, :, :, :, :, 0:128].reshape(128, 128).astype(F32)
+                r.vecs[:, b * 128 : (b + 1) * 128] = block.T[0:VROWS, :]
+            run_ticks(2)
+        elif name in ("projected", "self0", "self1", "self2", "self3"):
+            run_ticks(1)
+            if name == "self3":
+                run_ticks(1)
+        elif name == "cross_ready":
+            run_ticks(2)
+        elif name == "crossed":
+            run_ticks(len(ticks))
+            grad_in.wait()
+        elif name == "middle":
+            for g in gathers:
+                g.finish()
+            for copy in out_copies:
+                copy.wait()
+        elif name == "grads3":
+            j3.step0()
+        elif name == "grads2":
+            j2.step0()
+            j3.step1()
+        elif name == "grads1o":
+            j1o.step0()
+            j2.step1()
+            j3.step2()
+        elif name == "grads1":
+            j1.step0()
+        elif name == "grads0o":
+            j0o.step0()
+            j1.step1()
+        elif name == "grads0":
+            j0.step0()
+
+    plan = {
+        "cross_back": {2: [j3.step3, j2.step2], 5: [j3.step4, j2.step3], 8: [j2.step4, j1o.step1], 10: [j1o.step2], 12: [j1o.step3], 14: [j1o.step4]},
+        "self_back0": {0: [j0o.step1], 2: [j1.step2]},
+        "self_back1": {0: [j0o.step2], 2: [j1.step3]},
+        "self_back2": {0: [j0o.step3, j1.step4], 1: [j0o.step4]},
+    }
+
+    def at_step(name, t):
+        for when, actions in plan.get(name, {}).items():
+
+            @pl.when(t == when)
+            def _():
+                for action in actions:
+                    action()
+
+    r.get_out_grad = lambda i: r.db[rows_of(i), :]
+    out_copies = []
+
+    def put_layer_out(i, value):
+        for k in range(4):
+
+            @pl.when(i == k)
+            def _():
+                part = r.xt.at[(k // 2) * 256 : (k // 2) * 256 + 256, (k % 2) * 512 : (k % 2) * 512 + 512]
+                part[...] = value
+                pltpu.make_async_copy(part, layer_out.at[k * 256 : k * 256 + 256, :], l_sem.at[2 + k]).start()
+
+    for k in range(4):
+        part = r.xt.at[(k // 2) * 256 : (k // 2) * 256 + 256, (k % 2) * 512 : (k % 2) * 512 + 512]
+        out_copies.append(pltpu.make_async_copy(part, layer_out.at[k * 256 : k * 256 + 256, :], l_sem.at[2 + k]))
+    r.put_layer_out = put_layer_out
+
+    def memory_part(k):
+        return pltpu.make_async_copy(
+            r.gate.at[:, k * 512 : k * 512 + 512], memory_grad.at[k * 256 : k * 256 + 256, :], l_sem.at[6 + k]
+        )
+
+    def put_memory_grad(i, value):
+        for k in range(4):
+
+            @pl.when(i == k)
+            def _():
+                r.gate[:, k * 512 : k * 512 + 512] = value
+                memory_part(k).start()
+
+    r.put_memory_grad = put_memory_grad
+
+    def input_part(i, k):
+        return pltpu.make_async_copy(r.dz.at[rows_of(i), :], input_grad.at[rows_of(i), :], l_sem.at[10 + k])
+
+    def put_input_grad(i, value):
+        r.dz[rows_of(i), :] = value
+        for k in range(4):
+
+            @pl.when(i == k)
+            def _():
+                input_part(k, k).start()
+
+    r.put_input_grad = put_input_grad
+
+    run(r, emit, hook, at_step)
+
+    for k in range(4):
+        memory_part(k).wait()
+    moments_in = fetch(14, moments, r.gate.at[0:128, :])
+    weights_again = fetch(15, weights, r.gate.at[128:192, :])
+    sums = jnp.sum(r.vg[...], axis=1)
+    sums = jnp.concatenate([sums, jnp.zeros((128 - VROWS, 512), F32)], axis=0)
+    spread(
+        jnp.concatenate([sums[:, b * 128 : (b + 1) * 128].T for b in range(4)], axis=0),
+        r.vkeep, r.vgive, slice(0, 128),
+    )
+    jv.step0()
+    for name in ("step1", "step2", "step3", "step4"):
+        getattr(j0, name)()
+        getattr(jv, name)()
+
+    def square(i):
+        r.nsend[0] += jnp.broadcast_to(jnp.sum(r.own[pl.ds(pl.multiple_of(i * 8, 8), 8), :] ** 2), (8, 128))
+
+    r.nsend[0] = jnp.broadcast_to(jnp.sum(r.vown[...] * r.vown[...]), (8, 128))
+    loop(8, square)
+    sends = []
+    for n in range(1, 8):
+        sends.append(
+            pltpu.make_async_remote_copy(
+                src_ref=r.nsend.at[0], dst_ref=r.nrecv.at[n - 1], send_sem=n_send.at[n - 1], recv_sem=n_recv.at[n - 1],
+                device_id=p.in_plane(n), device_id_type=MESH,
+            )
+        )
+        sends[-1].start()
+    total = r.nsend[0]
+    for n in range(7):
+        sends[n].wait_recv()
+        total = total + r.nrecv[n]
+    r.nsend[1] = total
+    for d in range(1, 4):
+        sends.append(
+            pltpu.make_async_remote_copy(
+                src_ref=r.nsend.at[1], dst_ref=r.nrecv.at[6 + d], send_sem=n_send.at[6 + d], recv_sem=n_recv.at[6 + d],
+                device_id=p.along_z(d), device_id_type=MESH,
+            )
+        )
+        sends[-1].start()
+    for d in range(3):
+        sends[7 + d].wait_recv()
+        total = total + r.nrecv[7 + d]
+    norm = jnp.sqrt(total)
+    norm_out[...] = norm
+    factor = jnp.minimum(1.0, CLIP_NORM / (norm[0:1, 0:1] + 1e-06))
+    r.square[...] = jnp.zeros((128, 128), F32)
+    r.square[0:16, :] = r.vown[...]
+    vgrad = r.square[...].T[0:17, 0:16]
+    vec_out[...] = vgrad
+    vstep_out[...], vfirst_out[...], vsecond_out[...] = adam_parts(
+        vectors[...], vgrad, vector_moments[0], vector_moments[1], factor
+    )
+    moments_in.wait()
+    weights_again.wait()
+    puts = [pltpu.make_async_copy(r.own, mat_out, l_sem.at[16])]
+    puts[0].start()
+
+    def update(i):
+        a, b, c = (pl.ds(pl.multiple_of(i * 16 + o, 16), 16) for o in (0, 64, 128))
+        s, f, v = adam_parts(r.gate[c, :], r.own[a, :], r.gate[a, :], r.gate[b, :], factor)
+        r.gate[a, :] = f
+        r.gate[b, :] = v
+        r.gate[c, :] = s
+
+    loop(4, update)
+    for k, (ref, a) in enumerate(((first_out, 0), (second_out, 64), (step_out, 128))):
+        puts.append(pltpu.make_async_copy(r.gate.at[a : a + 64, :], ref, l_sem.at[17 + k]))
+        puts[-1].start()
+    for k in range(4):
+        input_part(k, k).wait()
+    for j in jobs:
+        j.finish()
+    for s in sends:
+        s.wait_send()
+    for s in puts:
+        s.wait()
+
+
+def fused_body(tokens, memory, target_lengths, source_lengths, out_grad, weights, vectors, weight_moments, vector_moments):
+    V = pl.BlockSpec(memory_space=pltpu.VMEM)
+    S = pl.BlockSpec(memory_space=pltpu.SMEM)
+    A = pl.BlockSpec(memory_space=pl.ANY)
+    mat = jax.ShapeDtypeStruct((64, 2048), F32)
+    vec_shape = jax.ShapeDtypeStruct(vectors.shape, F32)
+    big = jax.ShapeDtypeStruct(tokens.shape, F32)
+    layer_out, input_grad, memory_grad, norm, g, vg, st, vst, m1, m2, vm1, vm2 = pl.pallas_call(
+        fused_kernel,
+        out_shape=(
+            jax.ShapeDtypeStruct(tokens.shape, BF), big, big, jax.ShapeDtypeStruct((8, 128), F32),
+            mat, vec_shape, mat, vec_shape, mat, mat, vec_shape, vec_shape,
+        ),
+        in_specs=[S, S, V, V, A, A, V, A, V],
+        out_specs=(A, A, A, V, A, V, A, V, A, A, V, V),
+        scratch_shapes=[pltpu.VMEM(s, d) for _, s, d in SCRATCH + FUSED_SCRATCH]
+        + [
+            pltpu.SemaphoreType.DMA((N_GATHER, 10)),
+            pltpu.SemaphoreType.DMA((N_GATHER, 10)),
+            pltpu.SemaphoreType.DMA((N_REDUCE, 6)),
+            pltpu.SemaphoreType.DMA((N_REDUCE, 6)),
+            pltpu.SemaphoreType.DMA((10,)),
+            pltpu.SemaphoreType.DMA((10,)),
+            pltpu.SemaphoreType.DMA((20,)),
+        ],
+        compiler_params=pltpu.CompilerParams(vmem_limit_bytes=63400000, collective_id=0, has_side_effects=True),
+        name="layer",
+    )(
+        target_lengths, source_lengths, tokens, memory, out_grad, weights.reshape(64, 2048), vectors,
+        weight_moments.reshape(128, 2048), vector_moments,
+    )
+    back = lambda a: a.reshape(weights.shape)
+    return (layer_out, input_grad, memory_grad, norm[0, 0], back(g), vg, back(st), vst, back(m1), back(m2), vm1, vm2)
 
 
 def adam_update(params, grad_in, moments, factor):
@@ -492,8 +1031,9 @@
 def solution(mesh):
     both = ("dp", "shard")
     rows, mats, vecs = P(both, None), P(None, both, None), P(None, both)
+    fits = (mesh.shape["dp"], mesh.shape["shard"]) == (8, 4)
     return jax.shard_map(
-        generic_body,
+        fused_body if fits else generic_body,
         mesh=mesh,
         in_specs=(rows, rows, rows, rows, rows, mats, vecs, P(None, None, both, None), P(None, None, both)),
         out_specs=(rows, rows, rows, P(), mats, vecs, mats, vecs, mats, mats, vecs, vecs),

time: 671 us -> 275 us (0.41)
  waiting for transfers between devices: 350 us -> 0 us
  blocking collectives: 86.1 us -> 0 us
  Pallas kernels: 204 us -> 255 us
  between operations: 17 us -> 0.67 us
  local copies, waits for them, and re-layouts: 4.85 us -> 18.8 us
  other arithmetic: 7.95 us -> 0 us
    reduce_scatter x1 -> x0, waiting for transfers between devices: 180 us -> none  [generic_body(): lax.psum_scatter(mat_grad, axes, scatter_dimension=1, tiled=True)]
    unnamed x4 -> x0, waiting for transfers between devices: 132 us -> none
    pallas_call x1, Pallas kernels: 204 us -> 255 us  [fused_body(): pl.pallas_call(fused_kernel, out_shape=(jax.ShapeDtypeStruct(tokens.shape...]
    all_gather x1 -> x0, blocking collectives: 44 us -> none  [generic_body(): lax.all_gather(vectors.astype(BF), axes, axis=1, tiled=True).astype(F32)]
    psum x1 -> x0, blocking collectives: 42.1 us -> none  [generic_body(): grad_norm = jnp.sqrt(lax.psum(squares, axes))]
    all_gather x1 -> x0, waiting for transfers between devices: 37.1 us -> none  [generic_body(): w = lax.all_gather(weights.astype(BF), axes, axis=1, tiled=True)]
    unnamed x16 -> x25, local copies, waits for them, and re-layouts: 4.74 us -> 17.5 us
  transfers between devices with their start and end apart: 3 -> 0, of which waited for: 3 -> 0; matrix products, arithmetic and copies ran while one was open for 0% -> 0% of each run, Pallas kernels for 0% -> 0%
where the time goes in v2:
time: 275 us
  Pallas kernels  255 us (93%)
  local copies, waits for them, and re-layouts  18.8 us (7%)
    pallas_call x1, Pallas kernels, fused_body(): pl.pallas_call(fused_kernel, out_shape=(jax.ShapeDtypeStruct(tokens.shape...  255 us
    unnamed x25, local copies, waits for them, and re-layouts  17.5 us

profile of v2, /device:TPU:0, one launch (start us, length us, event | category | flops | bytes accessed | tf_op | source)
XLA Modules:
  0.0 274.7 jit_solution(7314551594294864153)
XLA Ops:
  0.6 1.4 copy.21.vectors
  2.0 1.4 copy.22.vector_moments
  3.4 255.2 %layer.1 = (bf16[1024,512]{1,0:T(8,128)(2,1)}, f32[1024,512]{1,0:T(8,128)}, f32[1024,512]{1,0:T(8,128)}, f32[8,128]{1,0:T(8,128)}, f32[64,2048]{1,0:T(8,128)}, /...) custom-call(s32[1,16]{1,0:T(1,128)} %tlen.1, ...), custom_call_target="tpu_custom_call" | custom-call | tf_op jit(solution)/shard_map/layer/pallas_call | solution.py:974
  258.7 0.0 copy-start.1
  258.7 1.3 slice.3
  260.0 1.4 copy.23
  261.4 1.4 copy.24
  262.8 1.4 copy.25
  264.1 1.4 copy.26
  265.5 2.3 copy.34
  267.8 0.0 copy-done.1
  267.8 0.0 copy-start
  267.8 1.3 copy.35
  269.1 1.0 copy-done
  270.1 0.0 copy-start.5
  270.1 0.0 copy-start.4
  270.1 1.3 copy.36
  271.4 0.1 copy-done.5
  271.5 0.0 copy-start.3
  271.5 0.0 copy-start.2
  271.5 0.8 copy.37
  272.3 0.0 copy-done.4
  272.3 0.8 copy.38
  273.1 0.0 copy-done.3
  273.1 0.8 copy.39
  273.9 0.0 copy-done.2
  273.9 0.8 copy.40
Async XLA Ops:
  258.7 9.1 %copy-start.1 = (f32[1024,512]{1,0:T(8,128)S(1)}, f32[1024,512]{1,0:T(8,128)}, u32[]{:S(2)}) copy-start(f32[1024,512]{1,0:T(8,128)} %get-tuple-element.61) | copy-start | bytes 6291460
  267.8 2.3 copy-start
  270.1 1.4 copy-start.5
  270.1 2.2 copy-start.4
  271.5 1.6 copy-start.3
  271.5 2.4 copy-start.2
